TPU v7x, 128 devices: a whole 4x4x4 slice. The times are simulated.
128 devices in a mesh: tm: 16 (over y, z_lo, core), space: 8 (over z_hi, x).
Axes of the slice: x: 4, y: 4, z: 4 (z_hi: 2, z_lo: 2; z = z_hi * 2 + z_lo), core: 2. Of those that a mesh axis runs over, the one named last changes fastest.
Arguments:
- tokens: bfloat16 [128, 256, 768], P('tm', 'space'), may hold values from -6 to 6
- x_weight: bfloat16 [768, 1536], replicated, may hold values from -0.21875 to 0.21875
- z_weight: bfloat16 [768, 1536], replicated, may hold values from -0.21875 to 0.21875
- bc_weight: bfloat16 [768, 256], replicated, may hold values from -0.21875 to 0.21875
- dt_weight: bfloat16 [768, 24], replicated, may hold values from -0.21875 to 0.21875
- conv_weight: float32 [2, 4, 1792], replicated, may hold values from -3 to 3
- conv_bias: float32 [2, 1792], replicated, may hold values from -1.8 to 1.8
- dt_bias: float32 [2, 24], replicated, may hold values from -4 to -1
- decay_rate: float32 [2, 24], replicated, may hold values from 1e-06 to 1
- skip_gain: float32 [2, 24], replicated, may hold values from 0.5 to 1.5
- norm_gain: float32 [1536], replicated, may hold values from 0.1 to 1.9
- out_weight: bfloat16 [1536, 768], replicated, may hold values from -0.15625 to 0.15625
Outputs:
- mixed: bfloat16 [128, 256, 768], P('tm', 'space')
All inputs are finite; a program needn't handle non-finite values.
Results may differ from a plain program's by a relative error of at most 0.0044.
The roundings to bfloat16 on the way count: a program that leaves them out, or rounds other values in their place, can miss the bound.
Values may be sent and summed in bfloat16 or wider, within the bound.
A program may use at most 448 MiB of HBM per device.

v0:
```python
import jax
import jax.numpy as jnp
from jax import lax
from jax.sharding import PartitionSpec as P

HEADS = 24
HEADDIM = 64
STATE = 128
KERNEL = 4
PATCH = 256


def carried_in(part, axis, combine, identity, reverse):
    count = lax.axis_size(axis)
    place = lax.axis_index(axis)
    ahead = count - 1 - place if reverse else place
    gathered = jax.tree.map(lambda a: lax.all_gather(a, axis), part)
    state = jax.tree.map(lambda a, e: jnp.zeros_like(a) + jnp.asarray(e, a.dtype), part, identity)

    def one(hop, state):
        source = count - 1 - hop if reverse else hop
        return combine(
            state, jax.tree.map(lambda a: lax.dynamic_index_in_dim(a, source, 0, False), gathered)
        )

    return lax.fori_loop(0, ahead, one, state)


def extended(block, sides, width):
    for axis, dim in sides:
        count = lax.axis_size(axis)
        forward = [(i, i + 1) for i in range(count - 1)]
        backward = [(target, source) for source, target in forward]
        low = lax.ppermute(
            lax.slice_in_dim(block, block.shape[dim] - width, None, axis=dim), axis, forward
        )
        high = lax.ppermute(lax.slice_in_dim(block, 0, width, axis=dim), axis, backward)
        block = jnp.concatenate([low, block, high], axis=dim)
    return block


def causal_mix(padded, kernel_taps, kernel_bias):
    length = padded.shape[0] - KERNEL + 1
    running = kernel_bias[None, :]
    for offset in range(KERNEL):
        running = running + kernel_taps[offset][None, :] * padded[offset : offset + length].astype(
            jnp.float32
        )
    return jax.nn.silu(running).astype(jnp.bfloat16)


def lower_table(length):
    rows = lax.broadcasted_iota(jnp.int32, (length, length), 0)
    cols = lax.broadcasted_iota(jnp.int32, (length, length), 1)
    return (rows >= cols).astype(jnp.float32)


def span_intra(x_blocks, b_blocks, c_blocks, step_sizes, prefix):
    scores = jnp.einsum("qin,qjn->qij", c_blocks, b_blocks, preferred_element_type=jnp.float32)
    prefix_heads = jnp.swapaxes(prefix, 1, 2)
    gaps = prefix_heads[:, :, :, None] - prefix_heads[:, :, None, :]
    block_len = prefix.shape[1]
    lower = lax.broadcasted_iota(jnp.int32, (block_len, block_len), 0) >= lax.broadcasted_iota(
        jnp.int32, (block_len, block_len), 1
    )
    decay = jnp.exp(jnp.where(lower, gaps, -jnp.inf))
    weights = (scores[:, None] * decay * jnp.swapaxes(step_sizes, 1, 2)[:, :, None, :]).astype(
        jnp.bfloat16
    )
    return jnp.einsum("qhij,qjhp->qihp", weights, x_blocks, preferred_element_type=jnp.float32)


def span_states(x_blocks, b_blocks, step_sizes, prefix):
    to_end = jnp.exp(prefix[:, -1:, :] - prefix)
    scaled = (x_blocks * (step_sizes * to_end)[..., None]).astype(jnp.bfloat16)
    return jnp.einsum("qlhp,qln->qhpn", scaled, b_blocks, preferred_element_type=jnp.float32)


def span_inter(c_blocks, entering, prefix):
    rounded = entering.astype(jnp.bfloat16)
    produced = jnp.einsum("qln,qhpn->qlhp", c_blocks, rounded, preferred_element_type=jnp.float32)
    return jnp.exp(prefix)[..., None] * produced


def combine_pairs(earlier, later):
    return (earlier[0] * later[0], later[0][:, None, None] * earlier[1] + later[1])


def entering_state(summary, reverse):
    neutral = (jnp.ones_like(summary[0]), jnp.zeros_like(summary[1]))
    before = carried_in(summary, ("tm", "space"), combine_pairs, neutral, reverse)
    return before[1]


def device_direction(conv_out, dt_rows, bias_row, rate_row, skip_row, reverse):
    row_count = conv_out.shape[0]
    blocks = row_count // PATCH
    x_blocks = conv_out[:, : HEADS * HEADDIM].reshape(blocks, PATCH, HEADS, HEADDIM)
    b_blocks = conv_out[:, HEADS * HEADDIM : HEADS * HEADDIM + STATE].reshape(blocks, PATCH, STATE)
    c_blocks = conv_out[:, HEADS * HEADDIM + STATE :].reshape(blocks, PATCH, STATE)
    step_sizes = jax.nn.softplus(dt_rows + bias_row[None, :]).reshape(blocks, PATCH, HEADS)
    prefix = jnp.einsum(
        "ij,cjh->cih",
        lower_table(PATCH),
        -rate_row[None, None, :] * step_sizes,
        precision=lax.Precision.HIGHEST,
    )
    intra = span_intra(x_blocks, b_blocks, c_blocks, step_sizes, prefix)
    states = span_states(x_blocks, b_blocks, step_sizes, prefix)
    block_totals = prefix[:, -1, :]
    through_blocks = jnp.dot(lower_table(blocks), block_totals, precision=lax.Precision.HIGHEST)
    before_blocks = through_blocks - block_totals
    earlier_mask = lax.broadcasted_iota(jnp.int32, (blocks, blocks), 0) > lax.broadcasted_iota(
        jnp.int32, (blocks, blocks), 1
    )
    carry_gaps = before_blocks[:, None, :] - through_blocks[None, :, :]
    carry_weights = jnp.exp(jnp.where(earlier_mask[:, :, None], carry_gaps, -jnp.inf))
    local_in = jnp.einsum("kch,chpn->khpn", carry_weights, states, precision=lax.Precision.HIGHEST)
    device_decay = jnp.exp(through_blocks[-1])
    end_weights = jnp.exp(through_blocks[-1][None, :] - through_blocks)
    device_end = jnp.einsum("ch,chpn->hpn", end_weights, states, precision=lax.Precision.HIGHEST)
    incoming = entering_state((device_decay, device_end), reverse)
    entering = local_in + jnp.exp(before_blocks)[:, :, None, None] * incoming[None]
    inter = span_inter(c_blocks, entering, prefix)
    produced = intra + inter + skip_row[None, None, :, None] * x_blocks
    return produced.reshape(row_count, HEADS * HEADDIM)


def body(
    tokens,
    x_weight,
    z_weight,
    bc_weight,
    dt_weight,
    conv_weight,
    conv_bias,
    dt_bias,
    decay_rate,
    skip_gain,
    norm_gain,
    out_weight,
):
    grouped = lax.all_to_all(tokens, "space", split_axis=0, concat_axis=1, tiled=True)
    frames_here = grouped.shape[0]
    sequence = grouped.reshape(frames_here * PATCH, grouped.shape[2])
    in_weight = jnp.concatenate([x_weight, bc_weight], axis=1)
    xbc = jnp.dot(sequence, in_weight, preferred_element_type=jnp.float32).astype(jnp.bfloat16)
    gate_z = jnp.dot(sequence, z_weight, preferred_element_type=jnp.float32)
    dt_raw = jnp.dot(sequence, dt_weight, preferred_element_type=jnp.float32)
    padded = extended(xbc, ((("tm", "space"), 0),), KERNEL - 1)
    forward_in = causal_mix(padded[: padded.shape[0] - (KERNEL - 1)], conv_weight[0], conv_bias[0])
    backward_in = causal_mix(padded[KERNEL - 1 :][::-1], conv_weight[1], conv_bias[1])
    y_forward = device_direction(forward_in, dt_raw, dt_bias[0], decay_rate[0], skip_gain[0], False)
    y_backward = device_direction(
        backward_in, dt_raw[::-1], dt_bias[1], decay_rate[1], skip_gain[1], True
    )[::-1]
    gated = (y_forward + y_backward) * jax.nn.silu(gate_z)
    scale = lax.rsqrt(jnp.mean(gated * gated, axis=-1, keepdims=True) + 1e-05)
    normed = (gated * scale * norm_gain[None, :]).astype(jnp.bfloat16)
    hidden = normed.reshape(frames_here, PATCH, normed.shape[1])
    returned = lax.all_to_all(hidden, "space", split_axis=1, concat_axis=0, tiled=True)
    mixed = jnp.einsum(
        "fpi,id->fpd", returned, out_weight, preferred_element_type=jnp.float32
    ).astype(jnp.bfloat16)
    return mixed


def solution(mesh):
    return jax.shard_map(
        body,
        mesh=mesh,
        in_specs=(P("tm", "space", None), P(), P(), P(), P(), P(), P(), P(), P(), P(), P(), P()),
        out_specs=P("tm", "space", None),
        check_vma=False,
    )
```

profile of v0, /device:TPU:57, one launch (start us, length us, event | category | flops | bytes accessed | tf_op | source)
XLA Modules:
  0.0 1515.5 jit_solution(2832961735654508357)
XLA Ops:
  6.5 6.6 all-to-all-start
  15.9 7.5 all-to-all-done
  24.1 2.8 fusion.21
  27.0 3.8 collective-permute-start.1
  32.9 8.9 slice.163
  43.1 3.0 copy.49
  48.0 13.9 slice.155
  61.9 13.9 slice.158
  75.9 13.9 slice.161
  89.8 3.2 multiply_convert_fusion.4
  97.2 2.7 broadcast_multiply_fusion
  104.8 3.0 copy.45
  112.2 2.7 broadcast_multiply_fusion.1
  115.6 64.5 %all-reduce.2 = (f32[3072]{0:T(1024)S(1)}, f32[3072]{0:T(1024)S(1)}) all-reduce(f32[3072]{0:T(1024)S(1)} %get-tuple-element.191, f32[3072]{0:T(1024)S(1)} %get-tuple-element.189), channel_id=2, replica_groups=mesh['tm'=16,'space'=8] {'tm','space'}, use_global_device_ids=true, to_apply=%add | all-reduce | flops 6144 | bytes 49152
  184.6 3.2 copy.51
  187.8 2.3 copy.48
  191.8 3.1 copy.47
  194.8 2.3 copy.44
  199.1 453.0 %all-gather.9.cloned.1.call-done = f32[3072,64,128]{2,1,0:T(8,128)} async-done(((f32[24,64,128]{2,1,0:T(8,128)}), f32[3072,64,128]{2,1,0:T(8,128)}) %all-gather.9.cloned.1.call-update) | async-done | bytes 100663312 | tf_op jit(solution)/shard_map/all_gather | solution.py:17
  652.1 14.4 while.27
  668.5 3.2 fusion.26
  671.6 3.1 copy.52
  674.7 12.8 rev.8
  687.5 518.9 %all-gather.7.cloned.1.call-done = f32[3072,64,128]{2,1,0:T(8,128)} async-done(((f32[24,64,128]{2,1,0:T(8,128)}), f32[3072,64,128]{2,1,0:T(8,128)}) %all-gather.7.cloned.1.call-update) | async-done | bytes 100663312 | tf_op jit(solution)/shard_map/all_gather | solution.py:17
  1206.5 243.8 %while.26 = (s32[]{:T(128)}, f32[24,64,128]{2,1,0:T(8,128)S(1)}, s32[]{:T(128)}, f32[128,24]{1,0:T(8,128)}, f32[128,24,64,128]{3,2,1,0:T(8,128)}, /*index=5*/s32[]{:T(128)}, s32[]{:T(128)}, s32[]{:T(128)}) while((s32[]{:T(128)}, f32[24,64,128]{2,1,0:T(8,128)S(1)}, s32[]{:T(128)}, f32[128,24]{1,0:T(8,128)}, f32[128,24,64,128]{3,2,1,0:T(8,128)}, ...), condition=%wide.region_1.2_spmd, body=%wide.region_0.1_spmd.sunk | while | flops 393221 | bytes 2359711 | solution.py:26
  1452.3 3.2 fusion.27
  1455.4 3.1 copy.53
  1458.5 2.9 multiply_reduce_fusion
  1461.7 2.4 copy.57
  1464.6 6.4 reduce.24
  1472.4 29.4 %all_to_all.21 = bf16[8,2,24576]{2,1,0:T(2,128)(2,1)S(1)} all-to-all(bf16[8,2,24576]{2,1,0:T(2,128)(2,1)} %reshape.349), channel_id=1, replica_groups=mesh['tm'=16,'space'=8] {'space'}, dimensions={0} | all-to-all | bytes 1572864 | tf_op jit(solution)/shard_map/all_to_all | solution.py:161
  1501.8 3.2 reshape.350
  (361 shorter events, 294.4 us)
Async XLA Ops:
  6.5 1452.0 %copy-start = (bf16[768,1536]{1,0:T(8,128)(2,1)S(1)}, bf16[768,1536]{1,0:T(8,128)(2,1)}, u32[]{:S(2)}) copy-start(bf16[768,1536]{1,0:T(8,128)(2,1)} %param.18) | copy-start | bytes 7077892
  6.5 16.9 %all-to-all-start = ((bf16[8,32,768]{2,1,0:T(8,128)(2,1)}), bf16[8,32,768]{2,1,0:T(8,128)(2,1)S(1)}, u32[]{:S(2)}, u32[]{:S(2)}) async-start(bf16[8,32,768]{2,1,0:T(8,128)(2,1)} %param.16), calls=%async_computation | async-start | bytes 786432 | tf_op jit(solution)/shard_map/all_to_all | solution.py:143
  13.1 638.9 %all-gather.9.cloned.1.call-start = ((), (), s32[]{:S(2)}) async-start(), calls=%async_computation.3 | async-start | bytes 101449728 | tf_op jit(solution)/shard_map/all_gather | solution.py:17
  23.4 0.7 copy-start.9
  24.1 6.7 copy-start.10
  24.1 6.7 copy-start.20
  27.0 19.1 %collective-permute-start.1 = (bf16[3,1792]{1,0:T(4,128)(2,1)S(1)}, bf16[3,1792]{1,0:T(4,128)(2,1)S(1)}, u32[]{:S(2)}, u32[]{:S(2)}) collective-permute-start(bf16[3,1792]{1,0:T(4,128)(2,1)S(1)} %get-tuple-element.174), channel_id=1, source_target_pairs={{1,0},{2,1},{3,2},{4,3},{5,4},{6,5},{7,6},{8,7},{9,8},{10,9},{11,1... | collective-permute-start | bytes 32264 | tf_op jit(solution)/shard_map/ppermute | solution.py:37
  89.8 4.1 copy-start.5
  92.9 0.9 copy-start.3
  100.0 1106.5 %all-gather.7.cloned.1.call-start = ((), (), s32[]{:S(2)}) async-start(), calls=%async_computation.2 | async-start | bytes 101449728 | tf_op jit(solution)/shard_map/all_gather | solution.py:17
  100.0 8.6 collective-permute-start
  102.2 0.7 copy-start.16
  107.9 3.0 copy-start.6
  109.9 0.9 copy-start.1
  112.2 3.4 copy-start.26
  112.2 70.8 %copy-start.4 = (bf16[256,1792]{1,0:T(8,128)(2,1)S(1)}, bf16[256,1792]{1,0:T(8,128)(2,1)}, u32[]{:S(2)}) copy-start(bf16[256,1792]{1,0:T(8,128)(2,1)} %copy-done.3) | copy-start | bytes 2752516
  184.6 5.5 copy-start.2
  666.5 1.8 copy-start.8
  666.5 1.9 copy-start.13
  666.5 1.9 copy-start.14
  666.5 1.9 copy-start.15
  666.6 1.9 copy-start.19
  666.6 1.9 copy-start.22
  666.6 1.9 copy-start.24
  1450.4 1.8 copy-start.7
  1450.4 1.9 copy-start.12
  1450.4 1.9 copy-start.17
  1450.4 1.9 copy-start.21
  1450.4 1.8 copy-start.23
  1455.4 3.1 copy-start.11
  1458.5 2.9 copy-start.25
  1505.0 2.1 copy-start.27
  (1 other events, 0.7 us)
Sparse Core Ops, SparseCore 0:
  100.1 551.8 all-gather.8
  653.7 552.6 all-gather.6
where the time goes:
time: 1530 us; the launch traced here: 1520 us
  waiting for transfers between devices  980 us (64%)
  local copies, waits for them, and re-layouts  198 us (13%)
  other arithmetic  188 us (12%)
  blocking collectives  93.9 us (6%)
  matrix products  25.1 us (2%)
    all_gather x2, waiting for transfers between devices, carried_in(): gathered = jax.tree.map(lambda a: lax.all_gather(a, axis), part)  972 us
    add x127, other arithmetic, combine_pairs(): later[0][:, None, None] * earlier[1] + later[1]  166 us
    mul x127, local copies, waits for them, and re-layouts, combine_pairs(): later[0][:, None, None] * earlier[1] + later[1]  87.6 us
    unnamed x1, blocking collectives  64.5 us
    slice x4, local copies, waits for them, and re-layouts, causal_mix(): padded[offset:offset + length].astype(jnp.float32)  50.7 us
  transfers between devices with their start and end apart: 5, of which 4 were waited for; matrix products, arithmetic and copies ran while one was open for 5% of the time, Pallas kernels for 0%

commit v1 on v0

v1 whole, which is shorter than its diff:
```python
import jax
import jax.numpy as jnp
from jax import lax
from jax.experimental import pallas as pl
from jax.experimental.pallas import tpu as pltpu
from jax.sharding import PartitionSpec as P

HEADS = 24
STATE = 128
PATCH = 256
D = 768
INNER = 1536
WIDE = INNER + 2 * STATE
HALF = INNER // 2
GROUP = 8
EDGE = 16
CHUNK = 256
LOG2E = 1.4426950408889634
F32, BF16 = jnp.float32, jnp.bfloat16
MESH = pl.DeviceIdType.MESH


def iota(shape, dim):
    return lax.broadcasted_iota(jnp.int32, shape, dim)


def split(a, parts):
    pieces = []
    for _ in range(parts):
        piece = a.astype(BF16)
        pieces.append(piece)
        a = a - piece.astype(F32)
    return jnp.concatenate(pieces, axis=1)


def dot(a, b):
    return jnp.dot(a, b, preferred_element_type=F32)


def silu(a):
    half = 0.5 * a
    return half + half * jnp.tanh(half)


def spread(parts, width, target):
    rows = iota((parts * 128, width), 0) & 127
    return (rows == target(iota((parts * 128, width), 1))).astype(F32).astype(BF16)


def pad_lanes(first, second):
    rows = first.shape[0]
    return jnp.concatenate([first, second, jnp.zeros((rows, 128 - 2 * HEADS), F32)], axis=1)


def kernel(
    tokens,
    x_weight,
    z_weight,
    bc_weight,
    dt_weight,
    conv_weight,
    conv_bias,
    dt_bias,
    decay_rate,
    skip_gain,
    norm_gain,
    out_weight,
    out,
    w_in,
    w_z,
    w_out,
    tok,
    xbc,
    conv_f,
    conv_b,
    b_turned,
    gate,
    y,
    scores,
    columns,
    q_rows,
    fac,
    ep,
    skip_rows,
    st,
    part_out,
    part_in,
    local,
    coef,
    coef_t,
    slab_out,
    slab_in,
    ent_out,
    ent_in,
    ent,
    log_mine,
    log_in,
    log_slab,
    log_slabs,
    mix,
    w_sem,
    tok_sem,
    tok_send,
    edge_send,
    log_send,
    log_recv,
    logt_send,
    logt_recv,
    pair_send,
    pair_recv,
    part_send,
    part_recv,
    slab_send,
    slab_recv,
    ent_send,
    ent_recv,
    epair_send,
    epair_recv,
    out_send,
    out_sem,
):
    tm = lax.axis_index("tm")
    s = lax.axis_index("space")
    slab = tm // 2
    c = tm % 2
    u = 2 * s + c
    corner_hi = jnp.logical_and(s == GROUP - 1, c == 1)
    corner_lo = jnp.logical_and(s == 0, c == 0)

    loads = [
        pltpu.make_async_copy(bc_weight, w_in.at[:, pl.ds(INNER, 2 * STATE)], w_sem.at[0]),
        pltpu.make_async_copy(x_weight, w_in.at[:, pl.ds(0, INNER)], w_sem.at[1]),
        pltpu.make_async_copy(z_weight, w_z, w_sem.at[2]),
        pltpu.make_async_copy(out_weight, w_out, w_sem.at[3]),
    ]
    for load in loads:
        load.start()

    barrier = pltpu.get_barrier_semaphore()

    def greet(d, _):
        v = lax.rem(u + d, 16)
        pl.semaphore_signal(barrier, inc=1, device_id=(2 * slab + v % 2, v // 2), device_id_type=MESH)
        return 0

    lax.fori_loop(1, 16, greet, 0)

    def greet_slab(d, _):
        t = lax.rem(slab + d, GROUP)
        pl.semaphore_signal(barrier, inc=1, device_id=(2 * t + c, s), device_id_type=MESH)
        return 0

    lax.fori_loop(1, GROUP, greet_slab, 0)
    above = lax.rem(slab + 1, GROUP)
    below = lax.rem(slab + GROUP - 1, GROUP)

    @pl.when(corner_hi)
    def _():
        pl.semaphore_signal(barrier, inc=1, device_id=(2 * above, 0), device_id_type=MESH)

    @pl.when(corner_lo)
    def _():
        pl.semaphore_signal(
            barrier, inc=1, device_id=(2 * below + 1, GROUP - 1), device_id_type=MESH
        )

    pl.semaphore_wait(barrier, 22 + jnp.logical_or(corner_hi, corner_lo).astype(jnp.int32))

    def send_tokens(j, action):
        ds, dc = 4 * c + j // 2, j % 2
        mine = jnp.logical_and(ds == s, dc == c)
        src, dst = tokens.at[j], tok.at[pl.ds(pl.multiple_of(EDGE + 32 * s, 16), 32)]

        @pl.when(jnp.logical_not(mine))
        def _():
            action(
                pltpu.make_async_remote_copy(
                    src, dst, tok_send.at[j], tok_sem, (2 * slab + dc, ds), MESH
                )
            )

        if action is started:

            @pl.when(mine)
            def _():
                pltpu.make_async_copy(src, dst, tok_sem).start()

    def send_edge(j, action, side):
        g = 8 * c + j + (1 if side == 0 else -1)
        ds, dc = lax.rem(g + 16, 16) // 2, lax.rem(g + 16, 16) % 2
        dt = lax.rem(slab + lax.div(g + 16, 16) - 1 + GROUP, GROUP)
        mine = jnp.logical_and(jnp.logical_and(ds == s, dc == c), dt == slab)
        src = tokens.at[j, pl.ds(16 if side == 0 else 0, EDGE)]
        dst = tok.at[pl.ds(0 if side == 0 else EDGE + PATCH, EDGE)]

        @pl.when(jnp.logical_not(mine))
        def _():
            action(
                pltpu.make_async_remote_copy(
                    src, dst, edge_send.at[side, j], tok_sem, (2 * dt + dc, ds), MESH
                )
            )

        if action is started:

            @pl.when(mine)
            def _():
                pltpu.make_async_copy(src, dst, tok_sem).start()

    def started(copy):
        copy.start()

    def left(copy):
        copy.wait_send()

    def all_tokens(action):
        def one(j, _):
            send_tokens(j, action)
            return 0

        lax.fori_loop(0, 8, one, 0)

        @pl.when(s == GROUP - 1)
        def _():
            def one(j, _):
                send_edge(j, action, 0)
                return 0

            lax.fori_loop(0, 8, one, 0)

        @pl.when(s == 0)
        def _():
            def one(j, _):
                send_edge(j, action, 1)
                return 0

            lax.fori_loop(0, 8, one, 0)

    all_tokens(started)

    skips = pad_lanes(skip_gain[0:1, :], skip_gain[1:2, :])
    for e in range(2):
        skip_rows[e : e + 1, :] = dot(
            split(jnp.broadcast_to(skips, (8, 128)), 3),
            spread(3, INNER, lambda l: HEADS * e + (l >> 6)),
        )[0:1, :]

    pltpu.make_async_copy(tok, tok, tok_sem).wait()

    @pl.when(jnp.logical_and(corner_lo, slab == 0))
    def _():
        tok[0:EDGE, :] = jnp.zeros((EDGE, D), BF16)

    @pl.when(jnp.logical_and(corner_hi, slab == GROUP - 1))
    def _():
        tok[EDGE + PATCH :, :] = jnp.zeros((EDGE, D), BF16)

    dt_raw = dot(tok[EDGE : EDGE + PATCH, :], dt_weight[...])
    step = jax.nn.softplus(
        pad_lanes(dt_raw, dt_raw) + pad_lanes(dt_bias[0:1, :], dt_bias[1:2, :])
    )
    rates = pad_lanes(decay_rate[0:1, :], decay_rate[1:2, :])
    rate_step = split(step * (rates * -LOG2E), 3)
    row, col = iota((PATCH, PATCH), 0), iota((PATCH, PATCH), 1)
    down = dot((row >= col).astype(F32).astype(BF16), rate_step)
    up = dot((row <= col).astype(F32).astype(BF16), rate_step)
    down = down[:, 0:128] + (down[:, 128:256] + down[:, 256:384])
    up = up[:, 0:128] + (up[:, 128:256] + up[:, 256:384])
    lane = iota((PATCH, 128), 1)
    prefix = jnp.where(lane < HEADS, down, up)
    total = jnp.where(lane[0:1] < HEADS, down[PATCH - 1 :, :], up[0:1, :])
    log_mine[...] = jnp.broadcast_to(total, (8, 128))
    log_in[u] = log_mine[...]

    def send_logs(d, _):
        v = lax.rem(u + d, 16)
        pltpu.make_async_remote_copy(
            log_mine,
            log_in.at[u],
            log_send.at[v],
            log_recv.at[u],
            (2 * slab + v % 2, v // 2),
            MESH,
        ).start()
        return 0

    lax.fori_loop(1, 16, send_logs, 0)

    columns[...] = split(prefix, 3)
    fac[...] = split(jnp.exp2(total - prefix) * step, 2)
    ep[...] = split(jnp.exp2(prefix), 2)
    q_rows[...] = (prefix - LOG2E * jnp.log(step)).T

    def convolved(offset):
        span = pl.ds(offset, CHUNK)
        xbc[...] = dot(tok[...], w_in[:, span]).astype(BF16).astype(F32)
        forward = conv_bias[0:1, span]
        backward = conv_bias[1:2, span]
        for k in range(4):
            forward = forward + conv_weight[0, k : k + 1, span] * xbc[pl.ds(EDGE - 3 + k, PATCH), :]
            backward = (
                backward + conv_weight[1, k : k + 1, span] * xbc[pl.ds(EDGE + 3 - k, PATCH), :]
            )
        forward, backward = silu(forward).astype(BF16), silu(backward).astype(BF16)
        conv_f[:, span] = forward
        conv_b[:, span] = backward
        return forward, backward

    loads[0].wait()
    both = convolved(INNER)
    for e in range(2):
        b_turned[e] = both[e][:, 0:STATE].astype(F32).T.astype(BF16)
    loads[1].wait()

    def pair_copy():
        return pltpu.make_async_remote_copy(
            st.at[2], st.at[c], pair_send, pair_recv, (2 * slab + 1 - c, s), MESH
        )

    def head_target(t):
        return lambda l: (l >> 6) + jnp.where(l < CHUNK, 4 * t, HEADS - 4 + 4 * t)

    def project(i, _):
        t = lax.rem((1 - c) * 3 + i, 6)
        x_f, x_b = convolved(pl.multiple_of(t * CHUNK, CHUNK))
        factor = dot(fac[...], spread(2, 2 * CHUNK, head_target(t)))
        slot = jnp.where(t // 3 == c, c, 2)
        place = pl.ds(pl.multiple_of((t % 3) * CHUNK, CHUNK), CHUNK)
        for e, x in ((0, x_f), (1, x_b)):
            scaled = (x.astype(F32) * factor[:, e * CHUNK : (e + 1) * CHUNK]).astype(BF16)
            st[slot, e, :, place] = dot(b_turned[e], scaled)

        @pl.when(i == 2)
        def _():
            pair_copy().start()

        return 0

    lax.fori_loop(0, 6, project, 0)

    def wait_logs(d, _):
        v = lax.rem(u + d, 16)
        pltpu.make_async_remote_copy(
            log_mine, log_in.at[v], log_send.at[v], log_recv.at[v], (tm, s), MESH
        ).wait_recv()
        return 0

    lax.fori_loop(1, 16, wait_logs, 0)
    chips = [log_in[2 * k][0:1, :] + log_in[2 * k + 1][0:1, :] for k in range(GROUP)]
    zero = jnp.zeros((1, 128), F32)
    before, after = [zero], [zero]
    for k in range(GROUP):
        before.append(before[-1] + chips[k])
        after.append(after[-1] + chips[GROUP - 1 - k])
    narrow = iota((1, 128), 1) < HEADS
    outside = [jnp.where(narrow, before[k], after[GROUP - 1 - k]) for k in range(GROUP)]
    log_slab[...] = jnp.broadcast_to(before[GROUP], (8, 128))
    log_slabs[slab] = log_slab[...]

    def slab_log_copy(t, source):
        return pltpu.make_async_remote_copy(
            log_slab, log_slabs.at[source], logt_send.at[t], logt_recv.at[source], (2 * t + c, s), MESH
        )

    def send_slab_logs(d, _):
        slab_log_copy(lax.rem(slab + d, GROUP), slab).start()
        return 0

    lax.fori_loop(1, GROUP, send_slab_logs, 0)

    half_target = lambda l: (l >> 6) + jnp.where(l < HALF, 12 * c, HEADS - 12 + 12 * c)
    table = jnp.concatenate(
        chips
        + outside
        + [log_in[2 * s][0:1, :], log_in[2 * s + 1][0:1, :]]
        + [jnp.zeros((6, 128), F32)],
        axis=0,
    )
    expand = spread(3, INNER, half_target)
    coef[...] = dot(split(jnp.exp2(table), 3), expand)

    pair_copy().wait_recv()
    d0, d1 = coef[16:17, :], coef[17:18, :]

    def part_copy(k, source):
        return pltpu.make_async_remote_copy(
            part_out.at[k],
            part_in.at[source],
            part_send.at[k],
            part_recv.at[source],
            (tm, k),
            MESH,
        )

    def combined(k):
        rows = pl.ds(pl.multiple_of(k * 16, 16), 16)
        return jnp.concatenate(
            [
                d1[:, :HALF] * st[0, 0, rows, :] + st[1, 0, rows, :],
                d0[:, HALF:] * st[1, 1, rows, :] + st[0, 1, rows, :],
            ],
            axis=1,
        ).astype(BF16)

    def send_part(d, _):
        k = lax.rem(s + d, GROUP)
        part_out[k] = combined(k)
        part_copy(k, s).start()
        return 0

    lax.fori_loop(1, GROUP, send_part, 0)
    part_in[s] = combined(s)

    for e, conv in ((0, conv_f), (1, conv_b)):
        scores[e] = lax.dot_general(
            conv[:, INNER + STATE :],
            conv[:, INNER : INNER + STATE],
            (((1,), (1,)), ((), ())),
            preferred_element_type=F32,
        )
    lower = iota((128, 128), 0) >= iota((128, 128), 1)
    upper = iota((128, 128), 0) <= iota((128, 128), 1)
    near = [
        (iota((1, 128), 1) < 64).astype(F32).astype(BF16),
        (iota((1, 128), 1) >= 64).astype(F32).astype(BF16),
    ]

    def weigh(e, i, j, column, line, mask):
        gap = column[128 * i : 128 * i + 128, :] - line[:, 128 * j : 128 * j + 128]
        if mask is not None:
            gap = jnp.where(mask, gap, -jnp.inf)
        return (
            scores[e, 128 * i : 128 * i + 128, 128 * j : 128 * j + 128] * jnp.exp2(gap)
        ).astype(BF16)

    def within(t, _):
        span = pl.ds(pl.multiple_of(t * 128, 128), 128)
        x_f, x_b = conv_f[:, span], conv_b[:, span]
        wide = dot(
            columns[...],
            spread(3, 512, lambda l: 2 * t + ((l >> 7) & 1) + jnp.where(l < 256, 0, HEADS)),
        )
        tops, bottoms, top_x, bottom_x = [], [], [], []
        for h in range(2):
            pf, pb = wide[:, 128 * h : 128 * h + 128], wide[:, 256 + 128 * h : 384 + 128 * h]
            qf, qb = q_rows[pl.ds(2 * t + h, 1), :], q_rows[pl.ds(HEADS + 2 * t + h, 1), :]
            tops += [
                weigh(0, 0, 0, pf, qf, lower),
                weigh(1, 0, 0, pb, qb, upper),
                weigh(1, 0, 1, pb, qb, None),
            ]
            bottoms += [
                weigh(0, 1, 0, pf, qf, None),
                weigh(0, 1, 1, pf, qf, lower),
                weigh(1, 1, 1, pb, qb, upper),
            ]
            xf, xb = x_f * near[h], x_b * near[h]
            top_x += [xf[0:128], xb]
            bottom_x += [xf, xb[128:256]]
        y[0:128, span] = dot(jnp.concatenate(tops, axis=1), jnp.concatenate(top_x, axis=0))
        y[128:256, span] = dot(jnp.concatenate(bottoms, axis=1), jnp.concatenate(bottom_x, axis=0))
        return 0

    def gate_columns(t, _):
        span = pl.ds(pl.multiple_of(t * CHUNK, CHUNK), CHUNK)
        gate[:, span] = silu(dot(tok[EDGE : EDGE + PATCH, :], w_z[:, span]))
        return 0

    loads[2].wait()
    lax.fori_loop(0, 6, gate_columns, 0)
    lax.fori_loop(0, 3, within, 0)

    def wait_part(d, _):
        k = lax.rem(s + d, GROUP)
        part_copy(k, k).wait_recv()
        return 0

    lax.fori_loop(1, GROUP, wait_part, 0)
    forward = jnp.zeros((16, HALF), F32)
    backward = jnp.zeros((16, HALF), F32)
    for k in range(GROUP):
        r = GROUP - 1 - k
        local[k, :, :HALF] = forward
        local[r, :, HALF:] = backward
        forward = coef[k : k + 1, :HALF] * forward + part_in[k, :, :HALF].astype(F32)
        backward = coef[r : r + 1, HALF:] * backward + part_in[r, :, HALF:].astype(F32)
    slab_out[...] = jnp.concatenate([forward, backward], axis=1).astype(BF16)

    def slab_copy(t, source):
        return pltpu.make_async_remote_copy(
            slab_out, slab_in.at[source], slab_send.at[t], slab_recv.at[source], (2 * t + c, s), MESH
        )

    def send_slab(d, _):
        slab_copy(lax.rem(slab + d, GROUP), slab).start()
        return 0

    lax.fori_loop(1, GROUP, send_slab, 0)
    slab_in[slab] = slab_out[...]

    lax.fori_loop(3, 8, within, 0)

    def wait_slab(d, _):
        t = lax.rem(slab + d, GROUP)
        slab_log_copy(t, t).wait_recv()
        slab_copy(t, t).wait_recv()
        return 0

    lax.fori_loop(1, GROUP, wait_slab, 0)
    table = jnp.concatenate([log_slabs[t][0:1, :] for t in range(GROUP)], axis=0)
    coef_t[...] = dot(split(jnp.exp2(table), 3), spread(3, INNER, half_target))
    forward = jnp.zeros((16, HALF), F32)
    backward = jnp.zeros((16, HALF), F32)
    for k in range(GROUP):
        r = GROUP - 1 - k
        forward = jnp.where(
            k < slab, coef_t[k : k + 1, :HALF] * forward + slab_in[k, :, :HALF].astype(F32), forward
        )
        backward = jnp.where(
            r > slab, coef_t[r : r + 1, HALF:] * backward + slab_in[r, :, HALF:].astype(F32), backward
        )
    come = jnp.concatenate([forward, backward], axis=1)

    def ent_copy(k, source):
        return pltpu.make_async_remote_copy(
            ent_out.at[k], ent_in.at[source], ent_send.at[k], ent_recv.at[source], (tm, k), MESH
        )

    def entering(k):
        return (local[k] + coef[pl.ds(GROUP + k, 1), :] * come).astype(BF16)

    def send_ent(d, _):
        k = lax.rem(s + d, GROUP)
        ent_out[k] = entering(k)
        ent_copy(k, s).start()
        return 0

    lax.fori_loop(1, GROUP, send_ent, 0)
    ent_in[s] = entering(s)

    lax.fori_loop(8, 12, within, 0)

    def wait_ent(d, _):
        k = lax.rem(s + d, GROUP)
        ent_copy(k, k).wait_recv()
        return 0

    lax.fori_loop(1, GROUP, wait_ent, 0)
    for k in range(GROUP):
        rows = slice(16 * k, 16 * k + 16)
        first, last = ent_in[k, :, :HALF], ent_in[k, :, HALF:]
        ent[0, 0, rows, :] = first
        ent[1, 1, rows, :] = last
        ent[1, 0, rows, :] = (d0[:, :HALF] * first.astype(F32) + st[0, 0, rows, :]).astype(BF16)
        ent[0, 1, rows, :] = (d1[:, HALF:] * last.astype(F32) + st[1, 1, rows, :]).astype(BF16)
    ent_pair = pltpu.make_async_remote_copy(
        ent.at[1 - c], ent.at[2], epair_send, epair_recv, (2 * slab + 1 - c, s), MESH
    )
    ent_pair.start()

    def finish(i, squares):
        t = lax.rem(c * 3 + i, 6)

        @pl.when(i == 3)
        def _():
            ent_pair.wait_recv()

        span = pl.ds(pl.multiple_of(t * CHUNK, CHUNK), CHUNK)
        slot = jnp.where(t // 3 == c, c, 2)
        place = pl.ds(pl.multiple_of((t % 3) * CHUNK, CHUNK), CHUNK)
        grow = dot(ep[...], spread(2, 2 * CHUNK, head_target(t)))
        total = y[:, span]
        for e, conv in ((0, conv_f), (1, conv_b)):
            total = total + grow[:, e * CHUNK : (e + 1) * CHUNK] * dot(
                conv[:, INNER + STATE :], ent[slot, e, :, place]
            )
            total = total + skip_rows[e : e + 1, span] * conv[:, span].astype(F32)
        gated = total * gate[:, span]
        y[:, span] = gated
        return squares + jnp.sum(gated * gated, axis=1, keepdims=True)

    squares = lax.fori_loop(0, 6, finish, jnp.zeros((PATCH, 1), F32))
    scale = lax.rsqrt(squares * (1.0 / INNER) + 1e-05)
    gains = norm_gain[...].reshape(1, INNER)
    loads[3].wait()

    core_home = s // 4
    slot_home = u - 8 * core_home

    def send_out(b, action):
        mine = jnp.logical_and(b == s, core_home == c)
        src, dst = mix.at[pl.ds(pl.multiple_of(32 * b, 32), 32)], out.at[slot_home]

        @pl.when(jnp.logical_not(mine))
        def _():
            action(
                pltpu.make_async_remote_copy(
                    src, dst, out_send.at[b], out_sem, (2 * slab + core_home, b), MESH
                )
            )

        if action is started:

            @pl.when(mine)
            def _():
                pltpu.make_async_copy(src, dst, out_sem).start()

    for half in range(2):
        rows = slice(128 * half, 128 * half + 128)
        normed = (y[rows, :] * scale[rows, :] * gains).astype(BF16)
        mix[rows, :] = dot(normed, w_out[...]).astype(BF16)
        for b in range(4 * half, 4 * half + 4):
            send_out(b, started)

    all_tokens(left)
    pair_copy().wait_send()
    ent_pair.wait_send()

    def wait_sent(d, _):
        v = lax.rem(u + d, 16)
        pltpu.make_async_remote_copy(
            log_mine, log_in.at[u], log_send.at[v], log_recv.at[u], (tm, s), MESH
        ).wait_send()
        return 0

    lax.fori_loop(1, 16, wait_sent, 0)

    def wait_sent_group(d, _):
        k = lax.rem(s + d, GROUP)
        part_copy(k, s).wait_send()
        ent_copy(k, s).wait_send()
        t = lax.rem(slab + d, GROUP)
        slab_log_copy(t, slab).wait_send()
        slab_copy(t, slab).wait_send()
        return 0

    lax.fori_loop(1, GROUP, wait_sent_group, 0)
    for b in range(8):
        send_out(b, left)
    pltpu.make_async_copy(out, out, out_sem).wait()


def body(*args):
    hbm = pl.BlockSpec(memory_space=pl.ANY)
    vmem = pl.BlockSpec(memory_space=pltpu.VMEM)
    dma = pltpu.SemaphoreType.DMA
    scratch = [
        pltpu.VMEM((D, WIDE), BF16),
        pltpu.VMEM((D, INNER), BF16),
        pltpu.VMEM((INNER, D), BF16),
        pltpu.VMEM((PATCH + 2 * EDGE, D), BF16),
        pltpu.VMEM((PATCH + 2 * EDGE, CHUNK), F32),
        pltpu.VMEM((PATCH, WIDE), BF16),
        pltpu.VMEM((PATCH, WIDE), BF16),
        pltpu.VMEM((2, STATE, PATCH), BF16),
        pltpu.VMEM((PATCH, INNER), F32),
        pltpu.VMEM((PATCH, INNER), F32),
        pltpu.VMEM((2, PATCH, PATCH), F32),
        pltpu.VMEM((PATCH, 384), BF16),
        pltpu.VMEM((128, PATCH), F32),
        pltpu.VMEM((PATCH, 256), BF16),
        pltpu.VMEM((PATCH, 256), BF16),
        pltpu.VMEM((8, INNER), F32),
        pltpu.VMEM((3, 2, STATE, HALF), F32),
        pltpu.VMEM((GROUP, 16, INNER), BF16),
        pltpu.VMEM((GROUP, 16, INNER), BF16),
        pltpu.VMEM((GROUP, 16, INNER), F32),
        pltpu.VMEM((24, INNER), F32),
        pltpu.VMEM((GROUP, INNER), F32),
        pltpu.VMEM((16, INNER), BF16),
        pltpu.VMEM((GROUP, 16, INNER), BF16),
        pltpu.VMEM((GROUP, 16, INNER), BF16),
        pltpu.VMEM((GROUP, 16, INNER), BF16),
        pltpu.VMEM((3, 2, STATE, HALF), BF16),
        pltpu.VMEM((8, 128), F32),
        pltpu.VMEM((16, 8, 128), F32),
        pltpu.VMEM((8, 128), F32),
        pltpu.VMEM((GROUP, 8, 128), F32),
        pltpu.VMEM((PATCH, D), BF16),
        dma((4,)),
        dma,
        dma((8,)),
        dma((2, 8)),
        dma((16,)),
        dma((16,)),
        dma((GROUP,)),
        dma((GROUP,)),
        dma,
        dma,
        dma((GROUP,)),
        dma((GROUP,)),
        dma((GROUP,)),
        dma((GROUP,)),
        dma((GROUP,)),
        dma((GROUP,)),
        dma,
        dma,
        dma((8,)),
        dma,
    ]
    return pl.pallas_call(
        kernel,
        out_shape=jax.ShapeDtypeStruct((8, 32, D), BF16),
        in_specs=[hbm] * 4 + [vmem] * 7 + [hbm],
        out_specs=hbm,
        scratch_shapes=scratch,
        compiler_params=pltpu.CompilerParams(
            collective_id=0, has_side_effects=True, vmem_limit_bytes=48 * 1024 * 1024
        ),
    )(*args)


def solution(mesh):
    return jax.shard_map(
        body,
        mesh=mesh,
        in_specs=(P("tm", "space", None),) + (P(),) * 11,
        out_specs=P("tm", "space", None),
        check_vma=False,
    )
```

time: 1530 us -> 70.9 us (0.05)
  the two profiles are of different devices: /device:TPU:57 before, /device:TPU:1 now
where the time goes in v1:
time: 70.9 us; the launch traced here: 70.4 us
  Pallas kernels  59.1 us (83%)
  local copies, waits for them, and re-layouts  11.3 us (16%)
    pallas_call x1, Pallas kernels, body(): pl.pallas_call(kernel, out_shape=jax.ShapeDtypeStruct((8, 32, D), BF16),...  59.1 us
    unnamed x22, local copies, waits for them, and re-layouts  11.3 us

profile of v1, /device:TPU:1, one launch (start us, length us, event | category | flops | bytes accessed | tf_op | source)
XLA Modules:
  0.0 70.4 jit_solution(1670723496177672760)
XLA Ops:
  0.0 0.9 %copy.13.dt_weight = bf16[768,24]{1,0:T(8,128)(2,1)S(1)} copy(bf16[768,24]{0,1:T(8,128)(2,1)} %param.16) | data formatting | bytes 73728 | tf_op args[4]
  0.9 0.0 copy-start
  0.9 1.7 %copy-done = bf16[768,1536]{1,0:T(8,128)(2,1)S(1)} copy-done((bf16[768,1536]{1,0:T(8,128)(2,1)S(1)}, bf16[768,1536]{1,0:T(8,128)(2,1)}, u32[]{:S(2)}) %copy-start) | copy-done | bytes 2359320
  2.6 0.0 copy-start.1
  2.6 1.7 %copy-done.1 = bf16[768,1536]{1,0:T(8,128)(2,1)S(1)} copy-done((bf16[768,1536]{1,0:T(8,128)(2,1)S(1)}, bf16[768,1536]{1,0:T(8,128)(2,1)}, u32[]{:S(2)}) %copy-start.1) | copy-done | bytes 2359320
  4.3 0.0 copy-start.2
  4.3 1.0 %copy-done.2 = bf16[8,32,768]{2,1,0:T(8,128)(2,1)S(1)} copy-done((bf16[8,32,768]{2,1,0:T(8,128)(2,1)S(1)}, bf16[8,32,768]{2,1,0:T(8,128)(2,1)}, u32[]{:S(2)}) %copy-start.2) | copy-done | bytes 393240
  5.3 0.0 copy-start.3
  5.3 1.0 %copy-done.3 = bf16[768,256]{1,0:T(8,128)(2,1)S(1)} copy-done((bf16[768,256]{1,0:T(8,128)(2,1)S(1)}, bf16[768,256]{1,0:T(8,128)(2,1)}, u32[]{:S(2)}) %copy-start.3) | copy-done | bytes 393240
  6.3 0.0 copy-start.4
  6.3 0.8 %copy-done.4 = f32[2,4,1792]{2,1,0:T(4,128)S(1)} copy-done((f32[2,4,1792]{2,1,0:T(4,128)S(1)}, f32[2,4,1792]{2,1,0:T(4,128)}, u32[]{:S(2)}) %copy-start.4) | copy-done | bytes 57368
  7.1 0.0 copy-start.5
  7.1 0.7 %copy-done.5 = f32[2,1792]{1,0:T(2,128)S(1)} copy-done((f32[2,1792]{1,0:T(2,128)S(1)}, f32[2,1792]{1,0:T(2,128)}, u32[]{:S(2)}) %copy-start.5) | copy-done | bytes 14360
  7.8 0.0 copy-start.6
  7.8 0.7 copy-done.6
  8.5 0.0 copy-start.7
  8.5 0.7 copy-done.7
  9.2 0.0 copy-start.8
  9.2 0.7 copy-done.8
  9.9 0.0 copy-start.9
  9.9 0.7 copy-done.9
  10.5 59.1 %shard_map.118 = bf16[8,32,768]{2,1,0:T(8,128)(2,1)S(1)} custom-call(bf16[8,32,768]{2,1,0:T(8,128)(2,1)S(1)} %copy-done.2, bf16[768,1536]{1,0:T(8,128)(2,1)S(1)} %copy-done, bf16[768,1536]{1,0:T(8,128)(2,1)S(1)} %copy-done.1, bf16[768,256]{1,0:T(8,128)(2,1)S(1)} %copy-done.3, bf16[768,24]{1,0:T(8,128)(2,1)S(1)} %copy.13.dt_weight, ...), custom_call_target="tpu_custom_call" | custom-call | tf_op jit(solution)/shard_map/pallas_call | solution.py:701
  69.7 0.7 %copy.15 = bf16[8,32,768]{2,1,0:T(8,128)(2,1)} copy(bf16[8,32,768]{2,1,0:T(8,128)(2,1)S(1)} %shard_map.118) | data formatting | bytes 786432
Async XLA Ops:
  0.9 1.7 %copy-start = (bf16[768,1536]{1,0:T(8,128)(2,1)S(1)}, bf16[768,1536]{1,0:T(8,128)(2,1)}, u32[]{:S(2)}) copy-start(bf16[768,1536]{1,0:T(8,128)(2,1)} %x_weight.1) | copy-start | bytes 7077892
  2.6 1.7 %copy-start.1 = (bf16[768,1536]{1,0:T(8,128)(2,1)S(1)}, bf16[768,1536]{1,0:T(8,128)(2,1)}, u32[]{:S(2)}) copy-start(bf16[768,1536]{1,0:T(8,128)(2,1)} %z_weight.1) | copy-start | bytes 7077892
  4.3 1.0 %copy-start.2 = (bf16[8,32,768]{2,1,0:T(8,128)(2,1)S(1)}, bf16[8,32,768]{2,1,0:T(8,128)(2,1)}, u32[]{:S(2)}) copy-start(bf16[8,32,768]{2,1,0:T(8,128)(2,1)} %tokens.1) | copy-start | bytes 1179652
  5.3 1.0 %copy-start.3 = (bf16[768,256]{1,0:T(8,128)(2,1)S(1)}, bf16[768,256]{1,0:T(8,128)(2,1)}, u32[]{:S(2)}) copy-start(bf16[768,256]{1,0:T(8,128)(2,1)} %bc_weight.1) | copy-start | bytes 1179652
  6.3 0.8 %copy-start.4 = (f32[2,4,1792]{2,1,0:T(4,128)S(1)}, f32[2,4,1792]{2,1,0:T(4,128)}, u32[]{:S(2)}) copy-start(f32[2,4,1792]{2,1,0:T(4,128)} %conv_weight.1) | copy-start | bytes 172036
  7.1 0.7 %copy-start.5 = (f32[2,1792]{1,0:T(2,128)S(1)}, f32[2,1792]{1,0:T(2,128)}, u32[]{:S(2)}) copy-start(f32[2,1792]{1,0:T(2,128)} %conv_bias.1) | copy-start | bytes 43012
  7.8 0.7 copy-start.6
  8.5 0.7 copy-start.7
  9.2 0.7 copy-start.8
  9.9 0.7 copy-start.9

commit v2 on v1

--- a/solution.py
+++ b/solution.py
@@ -57,6 +57,15 @@
     x_weight,
     z_weight,
     bc_weight,
+    dt_weight_hbm,
+    conv_weight_hbm,
+    conv_bias_hbm,
+    dt_bias_hbm,
+    decay_rate_hbm,
+    skip_gain_hbm,
+    norm_gain_hbm,
+    out_weight,
+    out,
     dt_weight,
     conv_weight,
     conv_bias,
@@ -64,8 +73,6 @@
     decay_rate,
     skip_gain,
     norm_gain,
-    out_weight,
-    out,
     w_in,
     w_z,
     w_out,
@@ -133,7 +140,21 @@
         pltpu.make_async_copy(z_weight, w_z, w_sem.at[2]),
         pltpu.make_async_copy(out_weight, w_out, w_sem.at[3]),
     ]
-    for load in loads:
+    small = [
+        pltpu.make_async_copy(source, target, w_sem.at[4 + at])
+        for at, (source, target) in enumerate(
+            (
+                (skip_gain_hbm, skip_gain),
+                (dt_weight_hbm, dt_weight),
+                (dt_bias_hbm, dt_bias),
+                (decay_rate_hbm, decay_rate),
+                (conv_weight_hbm, conv_weight),
+                (conv_bias_hbm, conv_bias),
+                (norm_gain_hbm, norm_gain),
+            )
+        )
+    ]
+    for load in small + loads:
         load.start()
 
     barrier = pltpu.get_barrier_semaphore()
@@ -238,6 +259,8 @@
 
     all_tokens(started)
 
+    for load in small:
+        load.wait()
     skips = pad_lanes(skip_gain[0:1, :], skip_gain[1:2, :])
     for e in range(2):
         skip_rows[e : e + 1, :] = dot(
@@ -255,7 +278,12 @@
     def _():
         tok[EDGE + PATCH :, :] = jnp.zeros((EDGE, D), BF16)
 
-    dt_raw = dot(tok[EDGE : EDGE + PATCH, :], dt_weight[...])
+    dt_raw = lax.dot_general(
+        tok[EDGE : EDGE + PATCH, :],
+        dt_weight[...],
+        (((1,), (1,)), ((), ())),
+        preferred_element_type=F32,
+    )
     step = jax.nn.softplus(
         pad_lanes(dt_raw, dt_raw) + pad_lanes(dt_bias[0:1, :], dt_bias[1:2, :])
     )
@@ -641,10 +669,17 @@
 
 
 def body(*args):
+    args = args[:4] + (args[4].T,) + args[5:]
     hbm = pl.BlockSpec(memory_space=pl.ANY)
-    vmem = pl.BlockSpec(memory_space=pltpu.VMEM)
     dma = pltpu.SemaphoreType.DMA
     scratch = [
+        pltpu.VMEM((HEADS, D), BF16),
+        pltpu.VMEM((2, 4, WIDE), F32),
+        pltpu.VMEM((2, WIDE), F32),
+        pltpu.VMEM((2, HEADS), F32),
+        pltpu.VMEM((2, HEADS), F32),
+        pltpu.VMEM((2, HEADS), F32),
+        pltpu.VMEM((INNER,), F32),
         pltpu.VMEM((D, WIDE), BF16),
         pltpu.VMEM((D, INNER), BF16),
         pltpu.VMEM((INNER, D), BF16),
@@ -677,7 +712,7 @@
         pltpu.VMEM((8, 128), F32),
         pltpu.VMEM((GROUP, 8, 128), F32),
         pltpu.VMEM((PATCH, D), BF16),
-        dma((4,)),
+        dma((11,)),
         dma,
         dma((8,)),
         dma((2, 8)),
@@ -701,11 +736,11 @@
     return pl.pallas_call(
         kernel,
         out_shape=jax.ShapeDtypeStruct((8, 32, D), BF16),
-        in_specs=[hbm] * 4 + [vmem] * 7 + [hbm],
+        in_specs=[hbm] * 12,
         out_specs=hbm,
         scratch_shapes=scratch,
         compiler_params=pltpu.CompilerParams(
-            collective_id=0, has_side_effects=True, vmem_limit_bytes=48 * 1024 * 1024
+            collective_id=0, has_side_effects=True, vmem_limit_bytes=60 * 1024 * 1024
         ),
     )(*args)
 

time: 70.9 us -> 61.2 us (0.86)
  local copies, waits for them, and re-layouts: 11.3 us -> 1.77 us
    unnamed x22 -> x1, local copies, waits for them, and re-layouts: 11.3 us -> 1.77 us
where the time goes in v2:
time: 61.2 us; the launch traced here: 61 us
  Pallas kernels  59.3 us (97%)
  local copies, waits for them, and re-layouts  1.77 us (3%)
    pallas_call x1, Pallas kernels, body(): pl.pallas_call(kernel, out_shape=jax.ShapeDtypeStruct((8, 32, D), BF16),...  59.3 us
    unnamed x1, local copies, waits for them, and re-layouts  1.77 us

profile of v2, /device:TPU:1, one launch (start us, length us, event | category | flops | bytes accessed | tf_op | source)
XLA Modules:
  0.0 61.0 jit_solution(15777694282993429552)
XLA Ops:
  0.0 59.3 %shard_map.118 = bf16[8,32,768]{2,1,0:T(8,128)(2,1)} custom-call(bf16[8,32,768]{2,1,0:T(8,128)(2,1)} %tokens.1, bf16[768,1536]{1,0:T(8,128)(2,1)} %x_weight.1, bf16[768,1536]{1,0:T(8,128)(2,1)} %z_weight.1, bf16[768,256]{1,0:T(8,128)(2,1)} %bc_weight.1, bf16[24,768]{1,0:T(8,128)(2,1)} %bitcast.1, f32[2,4,1792]{2,1,0:T(4,128)} %conv_weight_hbm.1, ...), custom_call_target="tpu_custom_call" | custom-call | tf_op jit(solution)/shard_map/pallas_call | solution.py:736
  59.3 1.8 %copy.14 = bf16[8,32,768]{2,1,0:T(8,128)(2,1)} copy(bf16[8,32,768]{2,1,0:T(8,128)(2,1)} %shard_map.118) | data formatting | bytes 786432

commit v3 on v2

--- a/solution.py
+++ b/solution.py
@@ -89,6 +89,9 @@
     fac,
     ep,
     skip_rows,
+    expand,
+    heads,
+    grow,
     st,
     part_out,
     part_in,
@@ -102,6 +105,8 @@
     ent,
     log_mine,
     log_in,
+    log_chip,
+    log_chips,
     log_slab,
     log_slabs,
     mix,
@@ -111,6 +116,8 @@
     edge_send,
     log_send,
     log_recv,
+    logc_send,
+    logc_recv,
     logt_send,
     logt_recv,
     pair_send,
@@ -235,8 +242,8 @@
         copy.wait_send()
 
     def all_tokens(action):
-        def one(j, _):
-            send_tokens(j, action)
+        def one(i, _):
+            send_tokens(lax.rem(s + i, 8), action)
             return 0
 
         lax.fori_loop(0, 8, one, 0)
@@ -261,12 +268,13 @@
 
     for load in small:
         load.wait()
+    half_target = lambda l: (l >> 6) + jnp.where(l < HALF, 12 * c, HEADS - 12 + 12 * c)
+    expand[...] = spread(3, INNER, half_target)
+    for e in range(2):
+        heads[e] = spread(3, INNER, lambda l: HEADS * e + (l >> 6))
     skips = pad_lanes(skip_gain[0:1, :], skip_gain[1:2, :])
     for e in range(2):
-        skip_rows[e : e + 1, :] = dot(
-            split(jnp.broadcast_to(skips, (8, 128)), 3),
-            spread(3, INNER, lambda l: HEADS * e + (l >> 6)),
-        )[0:1, :]
+        skip_rows[e : e + 1, :] = dot(split(jnp.broadcast_to(skips, (8, 128)), 3), heads[e])[0:1, :]
 
     pltpu.make_async_copy(tok, tok, tok_sem).wait()
 
@@ -298,21 +306,14 @@
     prefix = jnp.where(lane < HEADS, down, up)
     total = jnp.where(lane[0:1] < HEADS, down[PATCH - 1 :, :], up[0:1, :])
     log_mine[...] = jnp.broadcast_to(total, (8, 128))
-    log_in[u] = log_mine[...]
-
-    def send_logs(d, _):
-        v = lax.rem(u + d, 16)
-        pltpu.make_async_remote_copy(
-            log_mine,
-            log_in.at[u],
-            log_send.at[v],
-            log_recv.at[u],
-            (2 * slab + v % 2, v // 2),
-            MESH,
-        ).start()
-        return 0
-
-    lax.fori_loop(1, 16, send_logs, 0)
+    log_in[c] = log_mine[...]
+
+    def log_copy():
+        return pltpu.make_async_remote_copy(
+            log_mine, log_in.at[c], log_send, log_recv, (2 * slab + 1 - c, s), MESH
+        )
+
+    log_copy().start()
 
     columns[...] = split(prefix, 3)
     fac[...] = split(jnp.exp2(total - prefix) * step, 2)
@@ -345,17 +346,14 @@
             st.at[2], st.at[c], pair_send, pair_recv, (2 * slab + 1 - c, s), MESH
         )
 
-    def head_target(t):
-        return lambda l: (l >> 6) + jnp.where(l < CHUNK, 4 * t, HEADS - 4 + 4 * t)
-
     def project(i, _):
         t = lax.rem((1 - c) * 3 + i, 6)
         x_f, x_b = convolved(pl.multiple_of(t * CHUNK, CHUNK))
-        factor = dot(fac[...], spread(2, 2 * CHUNK, head_target(t)))
         slot = jnp.where(t // 3 == c, c, 2)
         place = pl.ds(pl.multiple_of((t % 3) * CHUNK, CHUNK), CHUNK)
         for e, x in ((0, x_f), (1, x_b)):
-            scaled = (x.astype(F32) * factor[:, e * CHUNK : (e + 1) * CHUNK]).astype(BF16)
+            factor = dot(fac[...], heads[e, 0:256, pl.ds(pl.multiple_of(t * CHUNK, CHUNK), CHUNK)])
+            scaled = (x.astype(F32) * factor).astype(BF16)
             st[slot, e, :, place] = dot(b_turned[e], scaled)
 
         @pl.when(i == 2)
@@ -366,46 +364,15 @@
 
     lax.fori_loop(0, 6, project, 0)
 
-    def wait_logs(d, _):
-        v = lax.rem(u + d, 16)
-        pltpu.make_async_remote_copy(
-            log_mine, log_in.at[v], log_send.at[v], log_recv.at[v], (tm, s), MESH
-        ).wait_recv()
-        return 0
-
-    lax.fori_loop(1, 16, wait_logs, 0)
-    chips = [log_in[2 * k][0:1, :] + log_in[2 * k + 1][0:1, :] for k in range(GROUP)]
-    zero = jnp.zeros((1, 128), F32)
-    before, after = [zero], [zero]
-    for k in range(GROUP):
-        before.append(before[-1] + chips[k])
-        after.append(after[-1] + chips[GROUP - 1 - k])
-    narrow = iota((1, 128), 1) < HEADS
-    outside = [jnp.where(narrow, before[k], after[GROUP - 1 - k]) for k in range(GROUP)]
-    log_slab[...] = jnp.broadcast_to(before[GROUP], (8, 128))
-    log_slabs[slab] = log_slab[...]
-
-    def slab_log_copy(t, source):
-        return pltpu.make_async_remote_copy(
-            log_slab, log_slabs.at[source], logt_send.at[t], logt_recv.at[source], (2 * t + c, s), MESH
-        )
-
-    def send_slab_logs(d, _):
-        slab_log_copy(lax.rem(slab + d, GROUP), slab).start()
-        return 0
-
-    lax.fori_loop(1, GROUP, send_slab_logs, 0)
-
-    half_target = lambda l: (l >> 6) + jnp.where(l < HALF, 12 * c, HEADS - 12 + 12 * c)
-    table = jnp.concatenate(
-        chips
-        + outside
-        + [log_in[2 * s][0:1, :], log_in[2 * s + 1][0:1, :]]
-        + [jnp.zeros((6, 128), F32)],
-        axis=0,
+    log_copy().wait_recv()
+    pair_logs = [log_in[0][0:1, :], log_in[1][0:1, :]]
+    chip_log = pair_logs[0] + pair_logs[1]
+    log_chip[...] = jnp.broadcast_to(chip_log, (8, 128))
+    log_chips[s] = log_chip[...]
+    coef[16:24, :] = dot(
+        split(jnp.exp2(jnp.concatenate(pair_logs + [jnp.zeros((6, 128), F32)], axis=0)), 3),
+        expand[...],
     )
-    expand = spread(3, INNER, half_target)
-    coef[...] = dot(split(jnp.exp2(table), 3), expand)
 
     pair_copy().wait_recv()
     d0, d1 = coef[16:17, :], coef[17:18, :]
@@ -437,6 +404,17 @@
         return 0
 
     lax.fori_loop(1, GROUP, send_part, 0)
+
+    def chip_log_copy(k, source):
+        return pltpu.make_async_remote_copy(
+            log_chip, log_chips.at[source], logc_send.at[k], logc_recv.at[source], (tm, k), MESH
+        )
+
+    def send_chip_logs(d, _):
+        chip_log_copy(lax.rem(s + d, GROUP), s).start()
+        return 0
+
+    lax.fori_loop(1, GROUP, send_chip_logs, 0)
     part_in[s] = combined(s)
 
     for e, conv in ((0, conv_f), (1, conv_b)):
@@ -485,18 +463,56 @@
             xf, xb = x_f * near[h], x_b * near[h]
             top_x += [xf[0:128], xb]
             bottom_x += [xf, xb[128:256]]
-        y[0:128, span] = dot(jnp.concatenate(tops, axis=1), jnp.concatenate(top_x, axis=0))
-        y[128:256, span] = dot(jnp.concatenate(bottoms, axis=1), jnp.concatenate(bottom_x, axis=0))
+        skip = skip_rows[0:1, span] * x_f.astype(F32) + skip_rows[1:2, span] * x_b.astype(F32)
+        y[0:128, span] = skip[0:128] + dot(jnp.concatenate(tops, axis=1), jnp.concatenate(top_x, axis=0))
+        y[128:256, span] = skip[128:256] + dot(jnp.concatenate(bottoms, axis=1), jnp.concatenate(bottom_x, axis=0))
         return 0
 
     def gate_columns(t, _):
         span = pl.ds(pl.multiple_of(t * CHUNK, CHUNK), CHUNK)
         gate[:, span] = silu(dot(tok[EDGE : EDGE + PATCH, :], w_z[:, span]))
+        for e in range(2):
+            grow[e, :, span] = dot(ep[...], heads[e, 0:256, span])
         return 0
 
     loads[2].wait()
     lax.fori_loop(0, 6, gate_columns, 0)
-    lax.fori_loop(0, 3, within, 0)
+
+    def wait_chip_logs(d, _):
+        k = lax.rem(s + d, GROUP)
+        chip_log_copy(k, k).wait_recv()
+        return 0
+
+    lax.fori_loop(1, GROUP, wait_chip_logs, 0)
+    chips = [log_chips[k][0:1, :] for k in range(GROUP)]
+    zero = jnp.zeros((1, 128), F32)
+    before, after = [zero], [zero]
+    for k in range(GROUP):
+        before.append(before[-1] + chips[k])
+        after.append(after[-1] + chips[GROUP - 1 - k])
+    narrow = iota((1, 128), 1) < HEADS
+    outside = [jnp.where(narrow, before[k], after[GROUP - 1 - k]) for k in range(GROUP)]
+    log_slab[...] = jnp.broadcast_to(before[GROUP], (8, 128))
+    log_slabs[slab] = log_slab[...]
+
+    def slab_log_copy(t, source):
+        return pltpu.make_async_remote_copy(
+            log_slab,
+            log_slabs.at[source],
+            logt_send.at[t],
+            logt_recv.at[source],
+            (2 * t + c, s),
+            MESH,
+        )
+
+    def send_slab_logs(d, _):
+        slab_log_copy(lax.rem(slab + d, GROUP), slab).start()
+        return 0
+
+    lax.fori_loop(1, GROUP, send_slab_logs, 0)
+    coef[0:16, :] = dot(
+        split(jnp.exp2(jnp.concatenate(chips + outside, axis=0)), 3), expand[...]
+    )
 
     def wait_part(d, _):
         k = lax.rem(s + d, GROUP)
@@ -512,11 +528,17 @@
         local[r, :, HALF:] = backward
         forward = coef[k : k + 1, :HALF] * forward + part_in[k, :, :HALF].astype(F32)
         backward = coef[r : r + 1, HALF:] * backward + part_in[r, :, HALF:].astype(F32)
-    slab_out[...] = jnp.concatenate([forward, backward], axis=1).astype(BF16)
+    slab_out[0] = forward.astype(BF16)
+    slab_out[1] = backward.astype(BF16)
 
     def slab_copy(t, source):
         return pltpu.make_async_remote_copy(
-            slab_out, slab_in.at[source], slab_send.at[t], slab_recv.at[source], (2 * t + c, s), MESH
+            slab_out.at[(t < slab).astype(jnp.int32)],
+            slab_in.at[source],
+            slab_send.at[t],
+            slab_recv.at[source],
+            (2 * t + c, s),
+            MESH,
         )
 
     def send_slab(d, _):
@@ -524,28 +546,34 @@
         return 0
 
     lax.fori_loop(1, GROUP, send_slab, 0)
-    slab_in[slab] = slab_out[...]
-
-    lax.fori_loop(3, 8, within, 0)
+    slab_in[slab] = slab_out[0]
+
+    lax.fori_loop(0, 5, within, 0)
+
+    def wait_slab_logs(d, _):
+        t = lax.rem(slab + d, GROUP)
+        slab_log_copy(t, t).wait_recv()
+        return 0
+
+    lax.fori_loop(1, GROUP, wait_slab_logs, 0)
+    table = jnp.concatenate([log_slabs[t][0:1, :] for t in range(GROUP)], axis=0)
+    coef_t[...] = dot(split(jnp.exp2(table), 3), expand[...])
 
     def wait_slab(d, _):
         t = lax.rem(slab + d, GROUP)
-        slab_log_copy(t, t).wait_recv()
         slab_copy(t, t).wait_recv()
         return 0
 
     lax.fori_loop(1, GROUP, wait_slab, 0)
-    table = jnp.concatenate([log_slabs[t][0:1, :] for t in range(GROUP)], axis=0)
-    coef_t[...] = dot(split(jnp.exp2(table), 3), spread(3, INNER, half_target))
     forward = jnp.zeros((16, HALF), F32)
     backward = jnp.zeros((16, HALF), F32)
     for k in range(GROUP):
         r = GROUP - 1 - k
         forward = jnp.where(
-            k < slab, coef_t[k : k + 1, :HALF] * forward + slab_in[k, :, :HALF].astype(F32), forward
+            k < slab, coef_t[k : k + 1, :HALF] * forward + slab_in[k].astype(F32), forward
         )
         backward = jnp.where(
-            r > slab, coef_t[r : r + 1, HALF:] * backward + slab_in[r, :, HALF:].astype(F32), backward
+            r > slab, coef_t[r : r + 1, HALF:] * backward + slab_in[r].astype(F32), backward
         )
     come = jnp.concatenate([forward, backward], axis=1)
 
@@ -566,7 +594,7 @@
     lax.fori_loop(1, GROUP, send_ent, 0)
     ent_in[s] = entering(s)
 
-    lax.fori_loop(8, 12, within, 0)
+    lax.fori_loop(5, 12, within, 0)
 
     def wait_ent(d, _):
         k = lax.rem(s + d, GROUP)
@@ -596,13 +624,9 @@
         span = pl.ds(pl.multiple_of(t * CHUNK, CHUNK), CHUNK)
         slot = jnp.where(t // 3 == c, c, 2)
         place = pl.ds(pl.multiple_of((t % 3) * CHUNK, CHUNK), CHUNK)
-        grow = dot(ep[...], spread(2, 2 * CHUNK, head_target(t)))
         total = y[:, span]
         for e, conv in ((0, conv_f), (1, conv_b)):
-            total = total + grow[:, e * CHUNK : (e + 1) * CHUNK] * dot(
-                conv[:, INNER + STATE :], ent[slot, e, :, place]
-            )
-            total = total + skip_rows[e : e + 1, span] * conv[:, span].astype(F32)
+            total = total + grow[e, :, span] * dot(conv[:, INNER + STATE :], ent[slot, e, :, place])
         gated = total * gate[:, span]
         y[:, span] = gated
         return squares + jnp.sum(gated * gated, axis=1, keepdims=True)
@@ -633,30 +657,26 @@
             def _():
                 pltpu.make_async_copy(src, dst, out_sem).start()
 
-    for half in range(2):
+    for turn in range(2):
+        half = turn
         rows = slice(128 * half, 128 * half + 128)
-        normed = (y[rows, :] * scale[rows, :] * gains).astype(BF16)
+        near_scale = scale[rows]
+        normed = (y[rows, :] * near_scale * gains).astype(BF16)
         mix[rows, :] = dot(normed, w_out[...]).astype(BF16)
-        for b in range(4 * half, 4 * half + 4):
-            send_out(b, started)
+        for i in range(4):
+            send_out(4 * half + i, started)
 
     all_tokens(left)
     pair_copy().wait_send()
     ent_pair.wait_send()
 
-    def wait_sent(d, _):
-        v = lax.rem(u + d, 16)
-        pltpu.make_async_remote_copy(
-            log_mine, log_in.at[u], log_send.at[v], log_recv.at[u], (tm, s), MESH
-        ).wait_send()
-        return 0
-
-    lax.fori_loop(1, 16, wait_sent, 0)
+    log_copy().wait_send()
 
     def wait_sent_group(d, _):
         k = lax.rem(s + d, GROUP)
         part_copy(k, s).wait_send()
         ent_copy(k, s).wait_send()
+        chip_log_copy(k, s).wait_send()
         t = lax.rem(slab + d, GROUP)
         slab_log_copy(t, slab).wait_send()
         slab_copy(t, slab).wait_send()
@@ -696,19 +716,24 @@
         pltpu.VMEM((PATCH, 256), BF16),
         pltpu.VMEM((PATCH, 256), BF16),
         pltpu.VMEM((8, INNER), F32),
+        pltpu.VMEM((384, INNER), BF16),
+        pltpu.VMEM((2, 384, INNER), BF16),
+        pltpu.VMEM((2, PATCH, INNER), F32),
         pltpu.VMEM((3, 2, STATE, HALF), F32),
         pltpu.VMEM((GROUP, 16, INNER), BF16),
         pltpu.VMEM((GROUP, 16, INNER), BF16),
         pltpu.VMEM((GROUP, 16, INNER), F32),
         pltpu.VMEM((24, INNER), F32),
         pltpu.VMEM((GROUP, INNER), F32),
-        pltpu.VMEM((16, INNER), BF16),
-        pltpu.VMEM((GROUP, 16, INNER), BF16),
+        pltpu.VMEM((2, 16, HALF), BF16),
+        pltpu.VMEM((GROUP, 16, HALF), BF16),
         pltpu.VMEM((GROUP, 16, INNER), BF16),
         pltpu.VMEM((GROUP, 16, INNER), BF16),
         pltpu.VMEM((3, 2, STATE, HALF), BF16),
         pltpu.VMEM((8, 128), F32),
-        pltpu.VMEM((16, 8, 128), F32),
+        pltpu.VMEM((2, 8, 128), F32),
+        pltpu.VMEM((8, 128), F32),
+        pltpu.VMEM((GROUP, 8, 128), F32),
         pltpu.VMEM((8, 128), F32),
         pltpu.VMEM((GROUP, 8, 128), F32),
         pltpu.VMEM((PATCH, D), BF16),
@@ -716,8 +741,10 @@
         dma,
         dma((8,)),
         dma((2, 8)),
-        dma((16,)),
-        dma((16,)),
+        dma,
+        dma,
+        dma((GROUP,)),
+        dma((GROUP,)),
         dma((GROUP,)),
         dma((GROUP,)),
         dma,

time: 61.2 us -> 59.2 us (0.967)
  Pallas kernels: 59.3 us -> 57.3 us
    pallas_call x1, Pallas kernels: 59.3 us -> 57.3 us  [body(): pl.pallas_call(kernel, out_shape=jax.ShapeDtypeStruct((8, 32, D), BF16),...]
where the time goes in v3:
time: 59.2 us; the launch traced here: 59.1 us
  Pallas kernels  57.3 us (97%)
  local copies, waits for them, and re-layouts  1.77 us (3%)
    pallas_call x1, Pallas kernels, body(): pl.pallas_call(kernel, out_shape=jax.ShapeDtypeStruct((8, 32, D), BF16),...  57.3 us
    unnamed x1, local copies, waits for them, and re-layouts  1.77 us

profile of v3, /device:TPU:1, one launch (start us, length us, event | category | flops | bytes accessed | tf_op | source)
XLA Modules:
  0.0 59.1 jit_solution(6817106864241843517)
XLA Ops:
  0.0 57.3 %shard_map.118 = bf16[8,32,768]{2,1,0:T(8,128)(2,1)} custom-call(bf16[8,32,768]{2,1,0:T(8,128)(2,1)} %tokens.1, bf16[768,1536]{1,0:T(8,128)(2,1)} %x_weight.1, bf16[768,1536]{1,0:T(8,128)(2,1)} %z_weight.1, bf16[768,256]{1,0:T(8,128)(2,1)} %bc_weight.1, bf16[24,768]{1,0:T(8,128)(2,1)} %bitcast.1, f32[2,4,1792]{2,1,0:T(4,128)} %conv_weight_hbm.1, ...), custom_call_target="tpu_custom_call" | custom-call | tf_op jit(solution)/shard_map/pallas_call | solution.py:763
  57.3 1.8 %copy.14 = bf16[8,32,768]{2,1,0:T(8,128)(2,1)} copy(bf16[8,32,768]{2,1,0:T(8,128)(2,1)} %shard_map.118) | data formatting | bytes 786432

commit v4 on v3

--- a/solution.py
+++ b/solution.py
@@ -138,6 +138,12 @@
     slab = tm // 2
     c = tm % 2
     u = 2 * s + c
+    far, at = 1 - s // 4, s % 4
+
+    def peer(d):
+        half = jnp.where(d <= 4, far, 1 - far)
+        return 4 * half + lax.rem(at + jnp.where(d <= 4, d - 1, d - 4), 4)
+
     corner_hi = jnp.logical_and(s == GROUP - 1, c == 1)
     corner_lo = jnp.logical_and(s == 0, c == 0)
 
@@ -192,6 +198,10 @@
             barrier, inc=1, device_id=(2 * below + 1, GROUP - 1), device_id_type=MESH
         )
 
+    half_target = lambda l: (l >> 6) + jnp.where(l < HALF, 12 * c, HEADS - 12 + 12 * c)
+    expand[...] = spread(3, INNER, half_target)
+    for e in range(2):
+        heads[e] = spread(3, INNER, lambda l: HEADS * e + (l >> 6))
     pl.semaphore_wait(barrier, 22 + jnp.logical_or(corner_hi, corner_lo).astype(jnp.int32))
 
     def send_tokens(j, action):
@@ -268,10 +278,6 @@
 
     for load in small:
         load.wait()
-    half_target = lambda l: (l >> 6) + jnp.where(l < HALF, 12 * c, HEADS - 12 + 12 * c)
-    expand[...] = spread(3, INNER, half_target)
-    for e in range(2):
-        heads[e] = spread(3, INNER, lambda l: HEADS * e + (l >> 6))
     skips = pad_lanes(skip_gain[0:1, :], skip_gain[1:2, :])
     for e in range(2):
         skip_rows[e : e + 1, :] = dot(split(jnp.broadcast_to(skips, (8, 128)), 3), heads[e])[0:1, :]
@@ -320,15 +326,15 @@
     ep[...] = split(jnp.exp2(prefix), 2)
     q_rows[...] = (prefix - LOG2E * jnp.log(step)).T
 
-    def convolved(offset):
+    def convolved(offset, turn):
         span = pl.ds(offset, CHUNK)
-        xbc[...] = dot(tok[...], w_in[:, span]).astype(BF16).astype(F32)
+        xbc[turn] = dot(tok[...], w_in[:, span]).astype(BF16).astype(F32)
         forward = conv_bias[0:1, span]
         backward = conv_bias[1:2, span]
         for k in range(4):
-            forward = forward + conv_weight[0, k : k + 1, span] * xbc[pl.ds(EDGE - 3 + k, PATCH), :]
+            forward = forward + conv_weight[0, k : k + 1, span] * xbc[turn, pl.ds(EDGE - 3 + k, PATCH), :]
             backward = (
-                backward + conv_weight[1, k : k + 1, span] * xbc[pl.ds(EDGE + 3 - k, PATCH), :]
+                backward + conv_weight[1, k : k + 1, span] * xbc[turn, pl.ds(EDGE + 3 - k, PATCH), :]
             )
         forward, backward = silu(forward).astype(BF16), silu(backward).astype(BF16)
         conv_f[:, span] = forward
@@ -336,7 +342,7 @@
         return forward, backward
 
     loads[0].wait()
-    both = convolved(INNER)
+    both = convolved(INNER, 6)
     for e in range(2):
         b_turned[e] = both[e][:, 0:STATE].astype(F32).T.astype(BF16)
     loads[1].wait()
@@ -346,9 +352,9 @@
             st.at[2], st.at[c], pair_send, pair_recv, (2 * slab + 1 - c, s), MESH
         )
 
-    def project(i, _):
+    def project(i):
         t = lax.rem((1 - c) * 3 + i, 6)
-        x_f, x_b = convolved(pl.multiple_of(t * CHUNK, CHUNK))
+        x_f, x_b = convolved(pl.multiple_of(t * CHUNK, CHUNK), i)
         slot = jnp.where(t // 3 == c, c, 2)
         place = pl.ds(pl.multiple_of((t % 3) * CHUNK, CHUNK), CHUNK)
         for e, x in ((0, x_f), (1, x_b)):
@@ -356,19 +362,28 @@
             scaled = (x.astype(F32) * factor).astype(BF16)
             st[slot, e, :, place] = dot(b_turned[e], scaled)
 
-        @pl.when(i == 2)
-        def _():
-            pair_copy().start()
-
-        return 0
-
-    lax.fori_loop(0, 6, project, 0)
+    for i in range(3):
+        project(i)
+    pair_copy().start()
+    for i in range(3, 6):
+        project(i)
 
     log_copy().wait_recv()
     pair_logs = [log_in[0][0:1, :], log_in[1][0:1, :]]
     chip_log = pair_logs[0] + pair_logs[1]
     log_chip[...] = jnp.broadcast_to(chip_log, (8, 128))
     log_chips[s] = log_chip[...]
+
+    def chip_log_copy(k, source):
+        return pltpu.make_async_remote_copy(
+            log_chip, log_chips.at[source], logc_send.at[k], logc_recv.at[source], (tm, k), MESH
+        )
+
+    def send_chip_logs(d, _):
+        chip_log_copy(lax.rem(s + d, GROUP), s).start()
+        return 0
+
+    lax.fori_loop(1, GROUP, send_chip_logs, 0)
     coef[16:24, :] = dot(
         split(jnp.exp2(jnp.concatenate(pair_logs + [jnp.zeros((6, 128), F32)], axis=0)), 3),
         expand[...],
@@ -398,23 +413,13 @@
         ).astype(BF16)
 
     def send_part(d, _):
-        k = lax.rem(s + d, GROUP)
+        k = peer(d)
         part_out[k] = combined(k)
         part_copy(k, s).start()
         return 0
 
     lax.fori_loop(1, GROUP, send_part, 0)
 
-    def chip_log_copy(k, source):
-        return pltpu.make_async_remote_copy(
-            log_chip, log_chips.at[source], logc_send.at[k], logc_recv.at[source], (tm, k), MESH
-        )
-
-    def send_chip_logs(d, _):
-        chip_log_copy(lax.rem(s + d, GROUP), s).start()
-        return 0
-
-    lax.fori_loop(1, GROUP, send_chip_logs, 0)
     part_in[s] = combined(s)
 
     for e, conv in ((0, conv_f), (1, conv_b)):
@@ -476,7 +481,7 @@
         return 0
 
     loads[2].wait()
-    lax.fori_loop(0, 6, gate_columns, 0)
+    lax.fori_loop(0, 3, gate_columns, 0)
 
     def wait_chip_logs(d, _):
         k = lax.rem(s + d, GROUP)
@@ -510,6 +515,7 @@
         return 0
 
     lax.fori_loop(1, GROUP, send_slab_logs, 0)
+    lax.fori_loop(3, 6, gate_columns, 0)
     coef[0:16, :] = dot(
         split(jnp.exp2(jnp.concatenate(chips + outside, axis=0)), 3), expand[...]
     )
@@ -586,7 +592,7 @@
         return (local[k] + coef[pl.ds(GROUP + k, 1), :] * come).astype(BF16)
 
     def send_ent(d, _):
-        k = lax.rem(s + d, GROUP)
+        k = peer(d)
         ent_out[k] = entering(k)
         ent_copy(k, s).start()
         return 0
@@ -614,28 +620,6 @@
     )
     ent_pair.start()
 
-    def finish(i, squares):
-        t = lax.rem(c * 3 + i, 6)
-
-        @pl.when(i == 3)
-        def _():
-            ent_pair.wait_recv()
-
-        span = pl.ds(pl.multiple_of(t * CHUNK, CHUNK), CHUNK)
-        slot = jnp.where(t // 3 == c, c, 2)
-        place = pl.ds(pl.multiple_of((t % 3) * CHUNK, CHUNK), CHUNK)
-        total = y[:, span]
-        for e, conv in ((0, conv_f), (1, conv_b)):
-            total = total + grow[e, :, span] * dot(conv[:, INNER + STATE :], ent[slot, e, :, place])
-        gated = total * gate[:, span]
-        y[:, span] = gated
-        return squares + jnp.sum(gated * gated, axis=1, keepdims=True)
-
-    squares = lax.fori_loop(0, 6, finish, jnp.zeros((PATCH, 1), F32))
-    scale = lax.rsqrt(squares * (1.0 / INNER) + 1e-05)
-    gains = norm_gain[...].reshape(1, INNER)
-    loads[3].wait()
-
     core_home = s // 4
     slot_home = u - 8 * core_home
 
@@ -657,14 +641,38 @@
             def _():
                 pltpu.make_async_copy(src, dst, out_sem).start()
 
+    def finish(i, rows, squares):
+        t = lax.rem(c * 3 + i, 6)
+        span = pl.ds(pl.multiple_of(t * CHUNK, CHUNK), CHUNK)
+        slot = jnp.where(t // 3 == c, c, 2)
+        place = pl.ds(pl.multiple_of((t % 3) * CHUNK, CHUNK), CHUNK)
+        total = y[rows, span]
+        for e, conv in ((0, conv_f), (1, conv_b)):
+            total = total + grow[e, rows, span] * dot(
+                conv[rows, INNER + STATE :], ent[slot, e, :, place]
+            )
+        gated = total * gate[rows, span]
+        y[rows, span] = gated
+        return squares + jnp.sum(gated * gated, axis=1, keepdims=True)
+
+    gains = norm_gain[...].reshape(1, INNER)
     for turn in range(2):
-        half = turn
-        rows = slice(128 * half, 128 * half + 128)
-        near_scale = scale[rows]
-        normed = (y[rows, :] * near_scale * gains).astype(BF16)
+        half = far if turn == 0 else 1 - far
+        rows = pl.ds(pl.multiple_of(128 * half, 128), 128)
+        squares = jnp.zeros((128, 1), F32)
+        for i in range(3):
+            squares = finish(i, rows, squares)
+        if turn == 0:
+            ent_pair.wait_recv()
+        for i in range(3, 6):
+            squares = finish(i, rows, squares)
+        scale = lax.rsqrt(squares * (1.0 / INNER) + 1e-05)
+        if turn == 0:
+            loads[3].wait()
+        normed = (y[rows, :] * scale * gains).astype(BF16)
         mix[rows, :] = dot(normed, w_out[...]).astype(BF16)
         for i in range(4):
-            send_out(4 * half + i, started)
+            send_out(4 * half + lax.rem(s + i, 4), started)
 
     all_tokens(left)
     pair_copy().wait_send()
@@ -704,7 +712,7 @@
         pltpu.VMEM((D, INNER), BF16),
         pltpu.VMEM((INNER, D), BF16),
         pltpu.VMEM((PATCH + 2 * EDGE, D), BF16),
-        pltpu.VMEM((PATCH + 2 * EDGE, CHUNK), F32),
+        pltpu.VMEM((7, PATCH + 2 * EDGE, CHUNK), F32),
         pltpu.VMEM((PATCH, WIDE), BF16),
         pltpu.VMEM((PATCH, WIDE), BF16),
         pltpu.VMEM((2, STATE, PATCH), BF16),

time: 59.2 us -> 56.5 us (0.954)
  Pallas kernels: 57.3 us -> 54.5 us
    pallas_call x1, Pallas kernels: 57.3 us -> 54.5 us  [body(): pl.pallas_call(kernel, out_shape=jax.ShapeDtypeStruct((8, 32, D), BF16),...]
where the time goes in v4:
time: 56.5 us; the launch traced here: 56.3 us
  Pallas kernels  54.5 us (96%)
  local copies, waits for them, and re-layouts  1.77 us (3%)
    pallas_call x1, Pallas kernels, body(): pl.pallas_call(kernel, out_shape=jax.ShapeDtypeStruct((8, 32, D), BF16),...  54.5 us
    unnamed x1, local copies, waits for them, and re-layouts  1.77 us

profile of v4, /device:TPU:1, one launch (start us, length us, event | category | flops | bytes accessed | tf_op | source)
XLA Modules:
  0.0 56.3 jit_solution(7185841706841226134)
XLA Ops:
  0.0 54.5 %shard_map.118 = bf16[8,32,768]{2,1,0:T(8,128)(2,1)} custom-call(bf16[8,32,768]{2,1,0:T(8,128)(2,1)} %tokens.1, bf16[768,1536]{1,0:T(8,128)(2,1)} %x_weight.1, bf16[768,1536]{1,0:T(8,128)(2,1)} %z_weight.1, bf16[768,256]{1,0:T(8,128)(2,1)} %bc_weight.1, bf16[24,768]{1,0:T(8,128)(2,1)} %bitcast.1, f32[2,4,1792]{2,1,0:T(4,128)} %conv_weight_hbm.1, ...), custom_call_target="tpu_custom_call" | custom-call | tf_op jit(solution)/shard_map/pallas_call | solution.py:771
  54.6 1.8 %copy.14 = bf16[8,32,768]{2,1,0:T(8,128)(2,1)} copy(bf16[8,32,768]{2,1,0:T(8,128)(2,1)} %shard_map.118) | data formatting | bytes 786432

commit v5 on v4

--- a/solution.py
+++ b/solution.py
@@ -53,7 +53,7 @@
 
 
 def kernel(
-    tokens,
+    tokens_hbm,
     x_weight,
     z_weight,
     bc_weight,
@@ -66,6 +66,7 @@
     norm_gain_hbm,
     out_weight,
     out,
+    tokens,
     dt_weight,
     conv_weight,
     conv_bias,
@@ -147,6 +148,8 @@
     corner_hi = jnp.logical_and(s == GROUP - 1, c == 1)
     corner_lo = jnp.logical_and(s == 0, c == 0)
 
+    fetch = pltpu.make_async_copy(tokens_hbm, tokens, w_sem.at[11])
+    fetch.start()
     loads = [
         pltpu.make_async_copy(bc_weight, w_in.at[:, pl.ds(INNER, 2 * STATE)], w_sem.at[0]),
         pltpu.make_async_copy(x_weight, w_in.at[:, pl.ds(0, INNER)], w_sem.at[1]),
@@ -202,6 +205,7 @@
     expand[...] = spread(3, INNER, half_target)
     for e in range(2):
         heads[e] = spread(3, INNER, lambda l: HEADS * e + (l >> 6))
+    fetch.wait()
     pl.semaphore_wait(barrier, 22 + jnp.logical_or(corner_hi, corner_lo).astype(jnp.int32))
 
     def send_tokens(j, action):
@@ -282,6 +286,8 @@
     for e in range(2):
         skip_rows[e : e + 1, :] = dot(split(jnp.broadcast_to(skips, (8, 128)), 3), heads[e])[0:1, :]
 
+    loads[0].wait()
+    loads[1].wait()
     pltpu.make_async_copy(tok, tok, tok_sem).wait()
 
     @pl.when(jnp.logical_and(corner_lo, slab == 0))
@@ -292,6 +298,24 @@
     def _():
         tok[EDGE + PATCH :, :] = jnp.zeros((EDGE, D), BF16)
 
+    def convolved(offset, turn):
+        span = pl.ds(offset, CHUNK)
+        xbc[turn] = dot(tok[...], w_in[:, span]).astype(BF16).astype(F32)
+        forward = conv_bias[0:1, span]
+        backward = conv_bias[1:2, span]
+        for k in range(4):
+            forward = forward + conv_weight[0, k : k + 1, span] * xbc[turn, pl.ds(EDGE - 3 + k, PATCH), :]
+            backward = (
+                backward + conv_weight[1, k : k + 1, span] * xbc[turn, pl.ds(EDGE + 3 - k, PATCH), :]
+            )
+        forward, backward = silu(forward).astype(BF16), silu(backward).astype(BF16)
+        conv_f[:, span] = forward
+        conv_b[:, span] = backward
+        return forward, backward
+
+    both = convolved(INNER, 6)
+    for e in range(2):
+        b_turned[e] = both[e][:, 0:STATE].astype(F32).T.astype(BF16)
     dt_raw = lax.dot_general(
         tok[EDGE : EDGE + PATCH, :],
         dt_weight[...],
@@ -326,27 +350,6 @@
     ep[...] = split(jnp.exp2(prefix), 2)
     q_rows[...] = (prefix - LOG2E * jnp.log(step)).T
 
-    def convolved(offset, turn):
-        span = pl.ds(offset, CHUNK)
-        xbc[turn] = dot(tok[...], w_in[:, span]).astype(BF16).astype(F32)
-        forward = conv_bias[0:1, span]
-        backward = conv_bias[1:2, span]
-        for k in range(4):
-            forward = forward + conv_weight[0, k : k + 1, span] * xbc[turn, pl.ds(EDGE - 3 + k, PATCH), :]
-            backward = (
-                backward + conv_weight[1, k : k + 1, span] * xbc[turn, pl.ds(EDGE + 3 - k, PATCH), :]
-            )
-        forward, backward = silu(forward).astype(BF16), silu(backward).astype(BF16)
-        conv_f[:, span] = forward
-        conv_b[:, span] = backward
-        return forward, backward
-
-    loads[0].wait()
-    both = convolved(INNER, 6)
-    for e in range(2):
-        b_turned[e] = both[e][:, 0:STATE].astype(F32).T.astype(BF16)
-    loads[1].wait()
-
     def pair_copy():
         return pltpu.make_async_remote_copy(
             st.at[2], st.at[c], pair_send, pair_recv, (2 * slab + 1 - c, s), MESH
@@ -701,6 +704,7 @@
     hbm = pl.BlockSpec(memory_space=pl.ANY)
     dma = pltpu.SemaphoreType.DMA
     scratch = [
+        pltpu.VMEM((8, 32, D), BF16),
         pltpu.VMEM((HEADS, D), BF16),
         pltpu.VMEM((2, 4, WIDE), F32),
         pltpu.VMEM((2, WIDE), F32),
@@ -745,7 +749,7 @@
         pltpu.VMEM((8, 128), F32),
         pltpu.VMEM((GROUP, 8, 128), F32),
         pltpu.VMEM((PATCH, D), BF16),
-        dma((11,)),
+        dma((12,)),
         dma,
         dma((8,)),
         dma((2, 8)),

time: 56.5 us -> 55.5 us (0.982)
  Pallas kernels: 54.5 us -> 53.6 us
    pallas_call x1, Pallas kernels: 54.5 us -> 53.6 us  [body(): pl.pallas_call(kernel, out_shape=jax.ShapeDtypeStruct((8, 32, D), BF16),...]
where the time goes in v5:
time: 55.5 us; the launch traced here: 55.4 us
  Pallas kernels  53.6 us (97%)
  local copies, waits for them, and re-layouts  1.77 us (3%)
    pallas_call x1, Pallas kernels, body(): pl.pallas_call(kernel, out_shape=jax.ShapeDtypeStruct((8, 32, D), BF16),...  53.6 us
    unnamed x1, local copies, waits for them, and re-layouts  1.77 us

profile of v5, /device:TPU:1, one launch (start us, length us, event | category | flops | bytes accessed | tf_op | source)
XLA Modules:
  0.0 55.4 jit_solution(16330662407260664102)
XLA Ops:
  0.0 53.6 %shard_map.118 = bf16[8,32,768]{2,1,0:T(8,128)(2,1)} custom-call(bf16[8,32,768]{2,1,0:T(8,128)(2,1)} %tokens_hbm.1, bf16[768,1536]{1,0:T(8,128)(2,1)} %x_weight.1, bf16[768,1536]{1,0:T(8,128)(2,1)} %z_weight.1, bf16[768,256]{1,0:T(8,128)(2,1)} %bc_weight.1, bf16[24,768]{1,0:T(8,128)(2,1)} %bitcast.1, f32[2,4,1792]{2,1,0:T(4,128)} %conv_weight_hbm.1, ...), custom_call_target="tpu_custom_call" | custom-call | tf_op jit(solution)/shard_map/pallas_call | solution.py:775
  53.6 1.8 %copy.14 = bf16[8,32,768]{2,1,0:T(8,128)(2,1)} copy(bf16[8,32,768]{2,1,0:T(8,128)(2,1)} %shard_map.118) | data formatting | bytes 786432

commit v6 on v5

--- a/solution.py
+++ b/solution.py
@@ -37,9 +37,12 @@
     return jnp.dot(a, b, preferred_element_type=F32)
 
 
+def silu_of_half(half):
+    return half + half * jnp.tanh(half)
+
+
 def silu(a):
-    half = 0.5 * a
-    return half + half * jnp.tanh(half)
+    return silu_of_half(0.5 * a)
 
 
 def spread(parts, width, target):
@@ -78,7 +81,6 @@
     w_z,
     w_out,
     tok,
-    xbc,
     conv_f,
     conv_b,
     b_turned,
@@ -298,22 +300,23 @@
     def _():
         tok[EDGE + PATCH :, :] = jnp.zeros((EDGE, D), BF16)
 
-    def convolved(offset, turn):
+    def convolved(offset):
         span = pl.ds(offset, CHUNK)
-        xbc[turn] = dot(tok[...], w_in[:, span]).astype(BF16).astype(F32)
-        forward = conv_bias[0:1, span]
-        backward = conv_bias[1:2, span]
+        wide = dot(tok[...], w_in[:, span]).astype(BF16).astype(F32)
+        forward = 0.5 * conv_bias[0:1, span]
+        backward = 0.5 * conv_bias[1:2, span]
+        taps = 0.5 * conv_weight[:, :, span]
         for k in range(4):
-            forward = forward + conv_weight[0, k : k + 1, span] * xbc[turn, pl.ds(EDGE - 3 + k, PATCH), :]
+            forward = forward + taps[0, k : k + 1] * pltpu.roll(wide, 3 - k, 0)[EDGE : EDGE + PATCH]
             backward = (
-                backward + conv_weight[1, k : k + 1, span] * xbc[turn, pl.ds(EDGE + 3 - k, PATCH), :]
+                backward + taps[1, k : k + 1] * pltpu.roll(wide, (PATCH + 2 * EDGE - 3 + k) % (PATCH + 2 * EDGE), 0)[EDGE : EDGE + PATCH]
             )
-        forward, backward = silu(forward).astype(BF16), silu(backward).astype(BF16)
+        forward, backward = silu_of_half(forward).astype(BF16), silu_of_half(backward).astype(BF16)
         conv_f[:, span] = forward
         conv_b[:, span] = backward
         return forward, backward
 
-    both = convolved(INNER, 6)
+    both = convolved(INNER)
     for e in range(2):
         b_turned[e] = both[e][:, 0:STATE].astype(F32).T.astype(BF16)
     dt_raw = lax.dot_general(
@@ -357,7 +360,7 @@
 
     def project(i):
         t = lax.rem((1 - c) * 3 + i, 6)
-        x_f, x_b = convolved(pl.multiple_of(t * CHUNK, CHUNK), i)
+        x_f, x_b = convolved(pl.multiple_of(t * CHUNK, CHUNK))
         slot = jnp.where(t // 3 == c, c, 2)
         place = pl.ds(pl.multiple_of((t % 3) * CHUNK, CHUNK), CHUNK)
         for e, x in ((0, x_f), (1, x_b)):
@@ -716,7 +719,6 @@
         pltpu.VMEM((D, INNER), BF16),
         pltpu.VMEM((INNER, D), BF16),
         pltpu.VMEM((PATCH + 2 * EDGE, D), BF16),
-        pltpu.VMEM((7, PATCH + 2 * EDGE, CHUNK), F32),
         pltpu.VMEM((PATCH, WIDE), BF16),
         pltpu.VMEM((PATCH, WIDE), BF16),
         pltpu.VMEM((2, STATE, PATCH), BF16),

time: 55.5 us -> 54.4 us (0.980)
  Pallas kernels: 53.6 us -> 52.5 us
    pallas_call x1, Pallas kernels: 53.6 us -> 52.5 us  [body(): pl.pallas_call(kernel, out_shape=jax.ShapeDtypeStruct((8, 32, D), BF16),...]
where the time goes in v6:
time: 54.4 us; the launch traced here: 54.3 us
  Pallas kernels  52.5 us (97%)
  local copies, waits for them, and re-layouts  1.77 us (3%)
    pallas_call x1, Pallas kernels, body(): pl.pallas_call(kernel, out_shape=jax.ShapeDtypeStruct((8, 32, D), BF16),...  52.5 us
    unnamed x1, local copies, waits for them, and re-layouts  1.77 us

profile of v6, /device:TPU:1, one launch (start us, length us, event | category | flops | bytes accessed | tf_op | source)
XLA Modules:
  0.0 54.3 jit_solution(11286900513443341100)
XLA Ops:
  0.0 52.5 %shard_map.118 = bf16[8,32,768]{2,1,0:T(8,128)(2,1)} custom-call(bf16[8,32,768]{2,1,0:T(8,128)(2,1)} %tokens_hbm.1, bf16[768,1536]{1,0:T(8,128)(2,1)} %x_weight.1, bf16[768,1536]{1,0:T(8,128)(2,1)} %z_weight.1, bf16[768,256]{1,0:T(8,128)(2,1)} %bc_weight.1, bf16[24,768]{1,0:T(8,128)(2,1)} %bitcast.1, f32[2,4,1792]{2,1,0:T(4,128)} %conv_weight_hbm.1, ...), custom_call_target="tpu_custom_call" | custom-call | tf_op jit(solution)/shard_map/pallas_call | solution.py:777
  52.5 1.8 %copy.14 = bf16[8,32,768]{2,1,0:T(8,128)(2,1)} copy(bf16[8,32,768]{2,1,0:T(8,128)(2,1)} %shard_map.118) | data formatting | bytes 786432

commit v7 on v6

--- a/solution.py
+++ b/solution.py
@@ -675,10 +675,12 @@
         scale = lax.rsqrt(squares * (1.0 / INNER) + 1e-05)
         if turn == 0:
             loads[3].wait()
-        normed = (y[rows, :] * scale * gains).astype(BF16)
-        mix[rows, :] = dot(normed, w_out[...]).astype(BF16)
-        for i in range(4):
-            send_out(4 * half + lax.rem(s + i, 4), started)
+        for q in range(2):
+            piece = pl.ds(pl.multiple_of(128 * half + 64 * q, 64), 64)
+            normed = (y[piece, :] * scale[64 * q : 64 * q + 64] * gains).astype(BF16)
+            mix[piece, :] = dot(normed, w_out[...]).astype(BF16)
+            for i in range(2):
+                send_out(4 * half + 2 * q + i, started)
 
     all_tokens(left)
     pair_copy().wait_send()

time: 54.4 us -> 54.2 us (level)
  no operation moved by 1% of the time
where the time goes in v7:
time: 54.2 us; the launch traced here: 54 us
  Pallas kernels  52.2 us (96%)
  local copies, waits for them, and re-layouts  1.77 us (3%)
    pallas_call x1, Pallas kernels, body(): pl.pallas_call(kernel, out_shape=jax.ShapeDtypeStruct((8, 32, D), BF16),...  52.2 us
    unnamed x1, local copies, waits for them, and re-layouts  1.77 us

profile of v7, /device:TPU:1, one launch (start us, length us, event | category | flops | bytes accessed | tf_op | source)
XLA Modules:
  0.0 54.0 jit_solution(6976556040390792439)
XLA Ops:
  0.0 52.2 %shard_map.118 = bf16[8,32,768]{2,1,0:T(8,128)(2,1)} custom-call(bf16[8,32,768]{2,1,0:T(8,128)(2,1)} %tokens_hbm.1, bf16[768,1536]{1,0:T(8,128)(2,1)} %x_weight.1, bf16[768,1536]{1,0:T(8,128)(2,1)} %z_weight.1, bf16[768,256]{1,0:T(8,128)(2,1)} %bc_weight.1, bf16[24,768]{1,0:T(8,128)(2,1)} %bitcast.1, f32[2,4,1792]{2,1,0:T(4,128)} %conv_weight_hbm.1, ...), custom_call_target="tpu_custom_call" | custom-call | tf_op jit(solution)/shard_map/pallas_call | solution.py:779
  52.3 1.8 %copy.14 = bf16[8,32,768]{2,1,0:T(8,128)(2,1)} copy(bf16[8,32,768]{2,1,0:T(8,128)(2,1)} %shard_map.118) | data formatting | bytes 786432
